TPU v7x, 512 devices: a whole 4x8x8 slice. The times are simulated.
512 devices in a mesh: row: 16 (over z_lo, x, core), col: 32 (over z_hi, y).
Axes of the slice: x: 4, y: 8, z: 8 (z_hi: 4, z_lo: 2; z = z_hi * 2 + z_lo), core: 2. Of those that a mesh axis runs over, the one named last changes fastest.
Arguments:
- ymatrix: bfloat16 [2048, 8, 128, 128], P(('row', 'col')), may hold values from -0.36 to 1.36
- zmatrix: bfloat16 [2048, 8, 128, 128], P(('row', 'col')), may hold values from -0.36 to 1.36
- pattern: int32 [2048, 8], P(('row', 'col')), may hold values 0 or 1
Outputs:
- y_update: bfloat16 [2048, 8, 128, 128], P(('row', 'col'))
- z_update: bfloat16 [2048, 8, 128, 128], P(('row', 'col'))
All inputs are finite; a program needn't handle non-finite values. No bound on the sum of `pattern` on one device may be relied on, other than what follows from the above.
Results may differ from a plain program's by a relative error of at most 0.008.
Values may be sent and summed in bfloat16 or wider, within the bound.
No kernel may reach another device: no remote copies, remote signals or barrier semaphores. Data moves between devices by JAX's collectives and lax.ppermute only.
A program may use at most 64 MiB of HBM per device.

v0:
```python
import jax
import jax.numpy as jnp
from jax import lax
from jax.sharding import PartitionSpec as P


def with_halo(cells, sides, width):
    for axis, dim in sides:
        count = lax.axis_size(axis)
        head = lax.slice_in_dim(cells, 0, width, axis=dim)
        tail = lax.slice_in_dim(cells, cells.shape[dim] - width, cells.shape[dim], axis=dim)
        cells = jnp.concatenate(
            [
                lax.ppermute(tail, axis, [(i, (i + 1) % count) for i in range(count)]),
                cells,
                lax.ppermute(head, axis, [((i + 1) % count, i) for i in range(count)]),
            ],
            axis=dim,
        )
    return cells


def band_product(left_side, right_ext):
    row_count, slot_count = (left_side.shape[0], left_side.shape[1])
    half_band = slot_count // 2
    right_pad = jnp.pad(right_ext, ((0, 0), (half_band, half_band), (0, 0), (0, 0)))
    running = jnp.zeros(left_side.shape, jnp.float32)
    for offset in range(slot_count):
        window = right_pad[
            offset : offset + row_count, slot_count - offset : 2 * slot_count - offset
        ]
        running = running + jnp.einsum(
            "rab,rdbc->rdac", left_side[:, offset], window, preferred_element_type=jnp.float32
        )
    return running


def local(ymatrix, zmatrix, pattern):
    row_count, slot_count = pattern.shape
    half_band = slot_count // 2
    block_size = ymatrix.shape[2]
    slot_index = lax.broadcasted_iota(jnp.int32, pattern.shape, 1)
    kept_mask = jnp.logical_or(pattern == 1, slot_index == half_band)[:, :, None, None]
    y_kept = jnp.where(kept_mask, ymatrix, jnp.zeros_like(ymatrix))
    z_kept = jnp.where(kept_mask, zmatrix, jnp.zeros_like(zmatrix))
    y_ext = with_halo(y_kept, ((("row", "col"), 0),), half_band)
    identity = jnp.eye(block_size, dtype=jnp.float32)
    diagonal_part = jnp.where(
        (slot_index == half_band)[:, :, None, None], 1.5 * identity, jnp.float32(0.0)
    )
    t_blocks = jnp.where(
        kept_mask, diagonal_part - 0.5 * band_product(z_kept, y_ext), jnp.float32(0.0)
    ).astype(jnp.bfloat16)
    z_ext = with_halo(z_kept, ((("row", "col"), 0),), half_band)
    z_update = jnp.where(kept_mask, band_product(t_blocks, z_ext), jnp.float32(0.0)).astype(
        jnp.bfloat16
    )
    t_ext = with_halo(t_blocks, ((("row", "col"), 0),), half_band)
    y_sums = band_product(y_kept, t_ext)
    y_update = jnp.where(kept_mask, y_sums, jnp.float32(0.0)).astype(jnp.bfloat16)
    return (y_update, z_update)


def solution(mesh):
    placed = (
        P(("row", "col"), None, None, None),
        P(("row", "col"), None, None, None),
        P(("row", "col"), None),
    )
    return jax.shard_map(
        local,
        mesh=mesh,
        in_specs=placed,
        out_specs=(P(("row", "col"), None, None, None), P(("row", "col"), None, None, None)),
        check_vma=False,
    )
```

profile of v0, /device:TPU:6, one launch (start us, length us, event | category | flops | bytes accessed | tf_op | source)
XLA Modules:
  0.0 164.4 jit_solution(11748190402292798916)
XLA Ops:
  0.6 0.7 compare_or_fusion
  1.3 0.1 copy.5
  1.4 1.7 %copy_select_fusion = (bf16[4,8,128,128]{3,2,0,1:T(8,128)(2,1)S(1)}, bf16[4,8,128,128]{3,2,0,1:T(8,128)(2,1)S(1)}) fusion(bf16[4,8,128,128]{3,2,1,0:T(8,128)(2,1)} %param.4, pred[4,8]{0,1:T(8,128)(4,1)S(1)} %copy.5, bf16[4,8,128,128]{3,2,1,0:T(8,128)(2,1)} %param.3), kind=kLoop, calls=%fused_computation.30 | loop fusion | flops 1048576 | bytes 4194336 | tf_op jit(solution)/shard_map/jit(_where)/select_n | solution.py:45
  3.2 3.5 %collective-permute-start = (bf16[4,8,128,128]{3,2,0,1:T(8,128)(2,1)S(1)}, bf16[4,8,128,128]{3,2,0,1:T(8,128)(2,1)S(1)}, u32[]{:S(2)}, u32[]{:S(2)}) collective-permute-start(bf16[4,8,128,128]{3,2,0,1:T(8,128)(2,1)S(1)} %get-tuple-element.5), channel_id=1, source_target_pairs={{0,1},{1,2},{2,3},{3,4},{4,5},{5,6},{6,7},{7,8},{8,9},{9,10},{10,1... | collective-permute-start | bytes 3145736 | tf_op jit(solution)/shard_map/ppermute | solution.py:14
  6.7 12.0 %collective-permute-start.1 = (bf16[4,8,128,128]{3,2,0,1:T(8,128)(2,1)S(1)}, bf16[4,8,128,128]{3,2,0,1:T(8,128)(2,1)S(1)}, u32[]{:S(2)}, u32[]{:S(2)}) collective-permute-start(bf16[4,8,128,128]{3,2,0,1:T(8,128)(2,1)S(1)} %get-tuple-element.5), channel_id=1, source_target_pairs={{1,0},{2,1},{3,2},{4,3},{5,4},{6,5},{7,6},{8,7},{9,8},{10,9},{11,1... | collective-permute-start | bytes 3145736 | tf_op jit(solution)/shard_map/ppermute | solution.py:16
  18.7 1.9 %collective-permute-start.4 = (bf16[4,8,128,128]{3,2,0,1:T(8,128)(2,1)S(1)}, bf16[4,8,128,128]{3,2,0,1:T(8,128)(2,1)S(1)}, u32[]{:S(2)}, u32[]{:S(2)}) collective-permute-start(bf16[4,8,128,128]{3,2,0,1:T(8,128)(2,1)S(1)} %get-tuple-element.4), channel_id=1, source_target_pairs={{0,1},{1,2},{2,3},{3,4},{4,5},{5,6},{6,7},{7,8},{8,9},{9,10},{10,1... | collective-permute-start | bytes 3145736 | tf_op jit(solution)/shard_map/ppermute | solution.py:14
  20.6 8.8 %collective-permute-start.5 = (bf16[4,8,128,128]{3,2,0,1:T(8,128)(2,1)S(1)}, bf16[4,8,128,128]{3,2,0,1:T(8,128)(2,1)S(1)}, u32[]{:S(2)}, u32[]{:S(2)}) collective-permute-start(bf16[4,8,128,128]{3,2,0,1:T(8,128)(2,1)S(1)} %get-tuple-element.4), channel_id=1, source_target_pairs={{1,0},{2,1},{3,2},{4,3},{5,4},{6,5},{7,6},{8,7},{9,8},{10,9},{11,1... | collective-permute-start | bytes 3145736 | tf_op jit(solution)/shard_map/ppermute | solution.py:16
  29.4 0.4 fusion.39
  29.8 32.1 %collective-permute-done = bf16[4,8,128,128]{3,2,0,1:T(8,128)(2,1)S(1)} collective-permute-done((bf16[4,8,128,128]{3,2,0,1:T(8,128)(2,1)S(1)}, bf16[4,8,128,128]{3,2,0,1:T(8,128)(2,1)S(1)}, u32[]{:S(2)}, u32[]{:S(2)}) %collective-permute-start) | collective-permute-done | bytes 1048608 | tf_op jit(solution)/shard_map/ppermute | solution.py:14
  62.0 0.0 collective-permute-done.1
  62.0 3.1 %fusion.5 = bf16[12,16,128,128]{3,2,0,1:T(8,128)(2,1)S(1)} fusion(bf16[4,8,128,128]{3,2,0,1:T(8,128)(2,1)S(1)} %collective-permute-done.1, bf16[4,8,128,128]{3,2,0,1:T(8,128)(2,1)S(1)} %get-tuple-element.5, bf16[4,8,128,128]{3,2,0,1:T(8,128)(2,1)S(1)} %collective-permute-done), kind=kLoop, calls=%fused_computation.7 | loop fusion | flops 37748736 | bytes 9437184 | tf_op jit(solution)/shard_map/concatenate | solution.py:12
  65.1 0.4 fusion.15
  65.5 0.4 fusion.17
  65.9 0.4 fusion.19
  66.4 0.4 fusion.21
  66.8 0.4 fusion.13
  67.2 0.4 fusion.11
  67.6 1.4 fusion.7
  69.0 1.9 %collective-permute-start.2 = (bf16[4,8,128,128]{3,2,0,1:T(8,128)(2,1)S(1)}, bf16[4,8,128,128]{3,2,0,1:T(8,128)(2,1)}, u32[]{:S(2)}, u32[]{:S(2)}) collective-permute-start(bf16[4,8,128,128]{3,2,0,1:T(8,128)(2,1)S(1)} %fusion.7), channel_id=1, source_target_pairs={{0,1},{1,2},{2,3},{3,4},{4,5},{5,6},{6,7},{7,8},{8,9},{9,10},{10,1... | collective-permute-start | bytes 3145736 | tf_op jit(solution)/shard_map/ppermute | solution.py:14
  71.0 11.3 %collective-permute-start.3 = (bf16[4,8,128,128]{3,2,0,1:T(8,128)(2,1)S(1)}, bf16[4,8,128,128]{3,2,0,1:T(8,128)(2,1)}, u32[]{:S(2)}, u32[]{:S(2)}) collective-permute-start(bf16[4,8,128,128]{3,2,0,1:T(8,128)(2,1)S(1)} %fusion.7), channel_id=1, source_target_pairs={{1,0},{2,1},{3,2},{4,3},{5,4},{6,5},{7,6},{8,7},{9,8},{10,9},{11,1... | collective-permute-start | bytes 3145736 | tf_op jit(solution)/shard_map/ppermute | solution.py:16
  82.2 0.5 fusion.26
  82.8 24.7 %collective-permute-done.4 = bf16[4,8,128,128]{3,2,0,1:T(8,128)(2,1)S(1)} collective-permute-done((bf16[4,8,128,128]{3,2,0,1:T(8,128)(2,1)S(1)}, bf16[4,8,128,128]{3,2,0,1:T(8,128)(2,1)S(1)}, u32[]{:S(2)}, u32[]{:S(2)}) %collective-permute-start.4) | collective-permute-done | bytes 1048608 | tf_op jit(solution)/shard_map/ppermute | solution.py:14
  107.5 0.0 collective-permute-done.5
  107.5 0.5 fusion.24
  107.9 0.5 fusion.25
  108.4 0.5 fusion.27
  109.0 0.5 fusion.28
  109.5 0.5 fusion.29
  109.9 0.5 fusion.30
  110.4 1.1 fusion.9
  111.5 1.3 copy.57
  112.8 0.5 fusion.34
  113.4 38.7 %collective-permute-done.2 = bf16[4,8,128,128]{3,2,0,1:T(8,128)(2,1)} collective-permute-done((bf16[4,8,128,128]{3,2,0,1:T(8,128)(2,1)S(1)}, bf16[4,8,128,128]{3,2,0,1:T(8,128)(2,1)}, u32[]{:S(2)}, u32[]{:S(2)}) %collective-permute-start.2) | collective-permute-done | bytes 1048608 | tf_op jit(solution)/shard_map/ppermute | solution.py:14
  152.1 0.0 collective-permute-done.3
  152.1 1.5 fusion.37
  153.6 1.5 fusion.38
  155.1 1.5 fusion.36
  156.6 1.4 fusion.35
  158.1 1.4 fusion.33
  159.5 1.5 fusion.32
  161.0 2.1 %fusion.8 = bf16[4,8,128,128]{2,3,0,1:T(8,128)(2,1)S(1)} fusion(f32[4,8,128,128]{3,2,0,1:T(8,128)S(1)} %fusion.32, f32[4,8,128,128]{3,2,0,1:T(8,128)S(1)} %fusion.33, f32[4,8,128,128]{3,2,0,1:T(8,128)S(1)} %fusion.34, f32[4,8,128,128]{3,2,0,1:T(8,128)S(1)} %fusion.35, f32[4,8,128,128]{3,2,0,1:T(8,128)S(1)} %fusion.36, f32[4,8,128,128]{3,2,0,1:T(8,128)S(1)} %fusion.38, ...), kind=kOutput, calls=%fused_computation.15 | convolution fusion | flops 98041856 | bytes 19006464 | tf_op jit(solution)/shard_map/rab,rdbc->rdac/dot_general | solution.py:32
  163.1 1.3 copy.56
  (2 shorter events, 0.0 us)
Async XLA Ops:
  3.2 58.8 %collective-permute-start = (bf16[4,8,128,128]{3,2,0,1:T(8,128)(2,1)S(1)}, bf16[4,8,128,128]{3,2,0,1:T(8,128)(2,1)S(1)}, u32[]{:S(2)}, u32[]{:S(2)}) collective-permute-start(bf16[4,8,128,128]{3,2,0,1:T(8,128)(2,1)S(1)} %get-tuple-element.5), channel_id=1, source_target_pairs={{0,1},{1,2},{2,3},{3,4},{4,5},{5,6},{6,7},{7,8},{8,9},{9,10},{10,1... | collective-permute-start | bytes 3145736 | tf_op jit(solution)/shard_map/ppermute | solution.py:14
  6.7 55.3 %collective-permute-start.1 = (bf16[4,8,128,128]{3,2,0,1:T(8,128)(2,1)S(1)}, bf16[4,8,128,128]{3,2,0,1:T(8,128)(2,1)S(1)}, u32[]{:S(2)}, u32[]{:S(2)}) collective-permute-start(bf16[4,8,128,128]{3,2,0,1:T(8,128)(2,1)S(1)} %get-tuple-element.5), channel_id=1, source_target_pairs={{1,0},{2,1},{3,2},{4,3},{5,4},{6,5},{7,6},{8,7},{9,8},{10,9},{11,1... | collective-permute-start | bytes 3145736 | tf_op jit(solution)/shard_map/ppermute | solution.py:16
  18.7 88.8 %collective-permute-start.4 = (bf16[4,8,128,128]{3,2,0,1:T(8,128)(2,1)S(1)}, bf16[4,8,128,128]{3,2,0,1:T(8,128)(2,1)S(1)}, u32[]{:S(2)}, u32[]{:S(2)}) collective-permute-start(bf16[4,8,128,128]{3,2,0,1:T(8,128)(2,1)S(1)} %get-tuple-element.4), channel_id=1, source_target_pairs={{0,1},{1,2},{2,3},{3,4},{4,5},{5,6},{6,7},{7,8},{8,9},{9,10},{10,1... | collective-permute-start | bytes 3145736 | tf_op jit(solution)/shard_map/ppermute | solution.py:14
  20.6 86.9 %collective-permute-start.5 = (bf16[4,8,128,128]{3,2,0,1:T(8,128)(2,1)S(1)}, bf16[4,8,128,128]{3,2,0,1:T(8,128)(2,1)S(1)}, u32[]{:S(2)}, u32[]{:S(2)}) collective-permute-start(bf16[4,8,128,128]{3,2,0,1:T(8,128)(2,1)S(1)} %get-tuple-element.4), channel_id=1, source_target_pairs={{1,0},{2,1},{3,2},{4,3},{5,4},{6,5},{7,6},{8,7},{9,8},{10,9},{11,1... | collective-permute-start | bytes 3145736 | tf_op jit(solution)/shard_map/ppermute | solution.py:16
  69.0 83.0 %collective-permute-start.2 = (bf16[4,8,128,128]{3,2,0,1:T(8,128)(2,1)S(1)}, bf16[4,8,128,128]{3,2,0,1:T(8,128)(2,1)}, u32[]{:S(2)}, u32[]{:S(2)}) collective-permute-start(bf16[4,8,128,128]{3,2,0,1:T(8,128)(2,1)S(1)} %fusion.7), channel_id=1, source_target_pairs={{0,1},{1,2},{2,3},{3,4},{4,5},{5,6},{6,7},{7,8},{8,9},{9,10},{10,1... | collective-permute-start | bytes 3145736 | tf_op jit(solution)/shard_map/ppermute | solution.py:14
  71.0 81.1 %collective-permute-start.3 = (bf16[4,8,128,128]{3,2,0,1:T(8,128)(2,1)S(1)}, bf16[4,8,128,128]{3,2,0,1:T(8,128)(2,1)}, u32[]{:S(2)}, u32[]{:S(2)}) collective-permute-start(bf16[4,8,128,128]{3,2,0,1:T(8,128)(2,1)S(1)} %fusion.7), channel_id=1, source_target_pairs={{1,0},{2,1},{3,2},{4,3},{5,4},{6,5},{7,6},{8,7},{9,8},{10,9},{11,1... | collective-permute-start | bytes 3145736 | tf_op jit(solution)/shard_map/ppermute | solution.py:16
where the time goes:
time: 167 us; the launch traced here: 164 us
  waiting for transfers between devices  95.5 us (57%)
  starting transfers between devices  39.3 us (24%)
  matrix products  20.4 us (12%)
  other arithmetic  5.58 us (3%)
  local copies, waits for them, and re-layouts  2.72 us (2%)
    ppermute x3, waiting for transfers between devices, with_halo(): lax.ppermute(tail, axis, [(i, (i + 1) % count) for i in range(count)])  95.5 us
    ppermute x3, starting transfers between devices, with_halo(): lax.ppermute(head, axis, [((i + 1) % count, i) for i in range(count)])  32 us
    dot_general x24, matrix products, band_product(): jnp.einsum('rab,rdbc->rdac', left_side[:, offset], window, preferred_elem...  20.4 us
    ppermute x3, starting transfers between devices, with_halo(): lax.ppermute(tail, axis, [(i, (i + 1) % count) for i in range(count)])  7.33 us
  transfers between devices with their start and end apart: 6, of which 3 were waited for; matrix products, arithmetic and copies ran while one was open for 8% of the time, Pallas kernels for 0%

commit v1 on v0

v1 whole, which is shorter than its diff:
```python
import jax
import jax.numpy as jnp
from jax import lax
from jax.experimental import pallas as pl
from jax.experimental.pallas import tpu as pltpu
from jax.sharding import PartitionSpec as P

AXES = ("row", "col")
B = 128
S = 512
RING = 8
BF = jnp.bfloat16
F32 = jnp.float32

LOWER = [(r, c) for r in range(4) for c in range(r, 4)]
UPPER = [(r, c) for r in range(4) for c in range(r)]
FULL = [(r, c) for r in range(4) for c in range(4)]


def of(name, blocks):
    return [(name, r, c) for r, c in blocks]


R1 = of("yU", UPPER)
L1 = of("yL", LOWER)
R2 = of("yD", FULL) + of("zU", UPPER[:3])
L2 = of("yD", [(r, c) for r in range(3) for c in range(3)])
R3 = of("zD", FULL) + of("zU", UPPER[3:])
L3 = of("zD", [(r, c) for r in range(3) for c in range(4)]) + of("zL", [p for p in LOWER if p[0] < 3])
L2, L3 = L2 + L3[-3:], L3[:-3]
COLUMN = {"L": 0, "D": S, "U": 2 * S}


def slot(part, r, c):
    return c - r + {"L": 0, "D": 4, "U": 8}[part]


def rows(i, n=1):
    return pl.ds(i * B, n * B)


def dot(a, b):
    return jnp.dot(a, b, preferred_element_type=F32)


def unpack(message, ref, into):
    for i, (name, r, c) in enumerate(message):
        target, row, column = into[name]
        target[pl.ds(row + r * B, B), pl.ds(column + c * B, B)] = ref[rows(i), :]


def keep(pattern, part, r, c):
    d = slot(part, r, c)
    return True if d == 4 else pattern[r, d] == 1


def masked(flag, block):
    return block if flag is True else jnp.where(flag, block, jnp.zeros_like(block))


def pack_kernel(pattern, y, z, r1, l1, r2, l2, r3, l3, yw, zw):
    for wide, source in ((yw, y), (zw, z)):
        for r in range(4):
            for d in range(8):
                k = True if d == 4 else pattern[r, d] == 1
                wide[rows(r), rows(r + d)] = masked(k, source[r, d])
            for c in range(12):
                if not r <= c < r + 8:
                    wide[rows(r), rows(c)] = jnp.zeros((B, B), BF)
    for message, ref in ((R1, r1), (L1, l1), (R2, r2), (L2, l2), (R3, r3), (L3, l3)):
        for i, (name, r, c) in enumerate(message):
            wide = yw if name[0] == "y" else zw
            ref[rows(i), :] = wide[rows(r), pl.ds(COLUMN[name[1]] + c * B, B)]
    line = lax.broadcasted_iota(jnp.int32, (16, B), 0)
    for message, ref in ((R1, r1), (L1, l1)):
        tile = jnp.zeros((16, B), F32)
        for i, (name, r, c) in enumerate(message):
            k = keep(pattern, name[1], r, c)
            tile = jnp.where(line == i, 1.0 if k is True else jnp.where(k, 1.0, 0.0), tile)
        ref[pl.ds(len(message) * B, 16), :] = tile.astype(BF)


def middle_kernel(pattern, yw, zw, r1, l1, td, e, l, column, acc, ud):
    column[pl.ds(0, S), :] = jnp.zeros((S, S), BF)
    column[pl.ds(2 * S, S), :] = jnp.zeros((S, S), BF)
    unpack(R1, r1, {"yU": (column, 0, 0)})
    unpack(L1, l1, {"yL": (column, 2 * S, 0)})
    column[pl.ds(S, S), :] = yw[:, pl.ds(S, S)]
    acc[...] = dot(zw[...], column[...])
    eye = jnp.where(
        lax.broadcasted_iota(jnp.int32, (B, B), 0) == lax.broadcasted_iota(jnp.int32, (B, B), 1), 1.5, 0.0
    )
    for r, c in FULL:
        block = -0.5 * acc[rows(r), rows(c)]
        if r == c:
            block = block + eye
        td[rows(r), rows(c)] = masked(keep(pattern, "D", r, c), block).astype(BF)
    acc[...] = dot(column[pl.ds(2 * S, S), :], td[...])
    for i, (r, c) in enumerate(LOWER):
        e[rows(i), :] = acc[rows(r), rows(c)].astype(BF)
    acc[...] = dot(column[pl.ds(0, S), :], td[...])
    for i, (r, c) in enumerate(UPPER):
        l[rows(i), :] = acc[rows(r), rows(c)].astype(BF)


def last_kernel(
    edge, pattern, yw, zw, td, r1, l1, r2, l2, r3, l3, r3b, l3b, e, l, yout, zout, yb, zb, tb, tw, side, acc
):
    for big in (yb, zb):
        big[pl.ds(0, S), :] = jnp.zeros((S, 3 * S), BF)
        big[pl.ds(2 * S, S), :] = jnp.zeros((S, 3 * S), BF)
    yb[pl.ds(S, S), :] = yw[...]
    zb[pl.ds(S, S), :] = zw[...]
    left = {"yD": (yb, 0, 0), "yU": (yb, 0, S), "zD": (zb, 0, 0), "zU": (zb, 0, S)}
    right = {"yL": (yb, 2 * S, S), "yD": (yb, 2 * S, 2 * S), "zL": (zb, 2 * S, S), "zD": (zb, 2 * S, 2 * S)}
    unpack(R1, r1, left)
    unpack(L1, l1, right)
    unpack(R2, r2, left)
    unpack(L2, l2, right)

    @pl.when(edge[0] == 1)
    def _():
        unpack(R3, r3b, left)

    @pl.when(edge[0] == 0)
    def _():
        unpack(R3, r3, left)

    @pl.when(edge[1] == 1)
    def _():
        unpack(L3, l3b, right)

    @pl.when(edge[1] == 0)
    def _():
        unpack(L3, l3, right)

    tw[...] = jnp.zeros((S, 3 * S), BF)
    tw[:, pl.ds(S, S)] = td[...]
    tb[...] = jnp.zeros((3 * S, S), BF)
    tb[pl.ds(S, S), :] = td[...]
    acc[...] = dot(zw[:, : 2 * S], yb[: 2 * S, :S])
    for r, c in LOWER:
        tw[rows(r), rows(c)] = masked(keep(pattern, "L", r, c), -0.5 * acc[rows(r), rows(c)]).astype(BF)
    acc[...] = dot(zw[:, S:], yb[S:, 2 * S :])
    for r, c in UPPER:
        tw[rows(r), pl.ds(2 * S + c * B, B)] = masked(
            keep(pattern, "U", r, c), -0.5 * acc[rows(r), rows(c)]
        ).astype(BF)
    left_mask = r1[pl.ds(len(R1) * B, 16), :].astype(F32)
    right_mask = l1[pl.ds(len(L1) * B, 16), :].astype(F32)
    acc[...] = dot(zb[:S, : 2 * S], yb[: 2 * S, S : 2 * S])
    for i, (r, c) in enumerate(UPPER):
        tb[rows(r), rows(c)] = (-0.5 * acc[rows(r), rows(c)] * left_mask[i : i + 1, :]).astype(BF)
    acc[...] = dot(zb[2 * S :, S:], yb[S:, S : 2 * S])
    for i, (r, c) in enumerate(LOWER):
        if r < 3:
            tb[pl.ds(2 * S + r * B, B), rows(c)] = (
                -0.5 * acc[rows(r), rows(c)] * right_mask[i : i + 1, :]
            ).astype(BF)

    def finish(out, part, blocks, extra=None):
        for i, (r, c) in enumerate(blocks):
            block = acc[rows(r), rows(c)]
            if extra is not None:
                block = block + extra[rows(i), :].astype(F32)
            out[r, slot(part, r, c)] = masked(keep(pattern, part, r, c), block).astype(BF)

    acc[...] = dot(tw[:, : 2 * S], zb[: 2 * S, :S])
    finish(zout, "L", LOWER)
    acc[...] = dot(tw[...], zb[:, S : 2 * S])
    finish(zout, "D", FULL)
    acc[...] = dot(tw[:, S:], zb[S:, 2 * S :])
    finish(zout, "U", UPPER)
    acc[...] = dot(yw[...], tb[...])
    finish(yout, "D", FULL)
    acc[...] = dot(yw[:, S : 2 * S], tw[:, :S])
    finish(yout, "L", LOWER, e)
    acc[...] = dot(yw[:, S : 2 * S], tw[:, 2 * S :])
    finish(yout, "U", UPPER, l)


VMEM = pl.BlockSpec(memory_space=pltpu.VMEM)
SMEM = pl.BlockSpec(memory_space=pltpu.SMEM)


def packed(message, masks=False):
    return jax.ShapeDtypeStruct((len(message) * B + 16 * masks, B), BF)


def call(kernel, outs, ins, scratch, flops, operands):
    outs = tuple(outs)
    moved = sum(v.size * v.dtype.itemsize for v in (*outs, *operands))
    return pl.pallas_call(
        kernel,
        out_shape=outs,
        in_specs=ins,
        out_specs=tuple(VMEM for _ in outs),
        scratch_shapes=scratch,
        compiler_params=pltpu.CompilerParams(vmem_limit_bytes=48 * 2**20),
        cost_estimate=pl.CostEstimate(flops=flops, bytes_accessed=moved, transcendentals=0),
    )(*operands)


def local(ymatrix, zmatrix, pattern):
    count = lax.axis_size("row") * lax.axis_size("col")
    place = lax.axis_index("col") % RING
    chain = [(i, (i + 1) % count) for i in range(count)]
    near = [p for p in chain if p[0] % RING != RING - 1]
    hop_z = [(i, (i + RING) % count) for i in range(count) if i % RING == RING - 1]
    hop_y = [(i, (i - RING + 1) % count) for i in range(count) if i % RING == RING - 1]

    def back(pairs):
        return [(b, a) for a, b in pairs]

    def flip(pairs):
        return [((count - 1 - a), (count - 1 - b)) for a, b in pairs]

    def send(x, pairs):
        return lax.ppermute(x, AXES, pairs)

    wide = jax.ShapeDtypeStruct((S, 3 * S), BF)
    r1, l1, r2, l2, r3, l3, yw, zw = call(
        pack_kernel,
        (packed(R1, True), packed(L1, True), packed(R2), packed(L2), packed(R3), packed(L3), wide, wide),
        [SMEM, VMEM, VMEM],
        [],
        0,
        (pattern, ymatrix, zmatrix),
    )
    r3z = send(r3, hop_z)
    l3z = send(l3, flip(hop_z))
    r1, l1 = send(r1, chain), send(l1, back(chain))
    r2, l2 = send(r2, chain), send(l2, back(chain))
    r3, l3 = send(r3, near), send(l3, back(near))
    r3b, l3b = send(r3z, hop_y), send(l3z, flip(hop_y))
    td, e, l = call(
        middle_kernel,
        (jax.ShapeDtypeStruct((S, S), BF), packed(LOWER), packed(UPPER)),
        [SMEM] + [VMEM] * 4,
        [pltpu.VMEM((3 * S, S), BF), pltpu.VMEM((S, S), F32), pltpu.VMEM((S, S), BF)],
        10 * S**3,
        (pattern, yw, zw, r1, l1),
    )
    e, l = send(e, chain), send(l, back(chain))
    edge = jnp.stack([place == 0, place == RING - 1]).astype(jnp.int32)
    whole = jax.ShapeDtypeStruct(ymatrix.shape, BF)
    return call(
        last_kernel,
        (whole, whole),
        [SMEM, SMEM] + [VMEM] * 13,
        [
            pltpu.VMEM((3 * S, 3 * S), BF),
            pltpu.VMEM((3 * S, 3 * S), BF),
            pltpu.VMEM((3 * S, S), BF),
            pltpu.VMEM((S, 3 * S), BF),
            pltpu.VMEM((S, S), BF),
            pltpu.VMEM((S, S), F32),
        ],
        40 * S**3,
        (edge, pattern, yw, zw, td, r1, l1, r2, l2, r3, l3, r3b, l3b, e, l),
    )


def solution(mesh):
    band = P(AXES, None, None, None)
    return jax.shard_map(
        local,
        mesh=mesh,
        in_specs=(band, band, P(AXES, None)),
        out_specs=(band, band),
        check_vma=False,
    )
```

time: 167 us -> 127 us (0.76)
  waiting for transfers between devices: 95.5 us -> 48.1 us
  matrix products: 20.4 us -> 0 us
  Pallas kernels: 0 us -> 15.9 us
  local copies, waits for them, and re-layouts: 2.72 us -> 13.3 us
  starting transfers between devices: 39.3 us -> 47.2 us
  other arithmetic: 5.58 us -> 0.08 us
    ppermute x6 -> x12, waiting for transfers between devices: 95.5 us -> 48.1 us  [send(): return lax.ppermute(x, AXES, pairs)]
    dot_general x24 -> x0, matrix products: 20.4 us -> none  [band_product(): jnp.einsum('rab,rdbc->rdac', left_side[:, offset], window, preferred_elem...]
    pallas_call x0 -> x3, Pallas kernels: none -> 15.9 us  [call(): pl.pallas_call(kernel, out_shape=outs, in_specs=ins, out_specs=tuple((VME...]
    unnamed x2 -> x32, local copies, waits for them, and re-layouts: 2.63 us -> 13.3 us
    ppermute x6 -> x12, starting transfers between devices: 39.3 us -> 47.2 us  [send(): return lax.ppermute(x, AXES, pairs)]
    concatenate x1 -> x0, other arithmetic: 3.13 us -> none  [with_halo(): jnp.concatenate([lax.ppermute(tail, axis, [(i, (i + 1) % count) for i in...]
    select_n x1 -> x0, other arithmetic: 1.74 us -> none  [local(): z_kept = jnp.where(kept_mask, zmatrix, jnp.zeros_like(zmatrix))]
  transfers between devices with their start and end apart: 6 -> 12, of which waited for: 3 -> 4; matrix products, arithmetic and copies ran while one was open for 8% -> 0% of each run, Pallas kernels for 0% -> 2%
where the time goes in v1:
time: 127 us; the launch traced here: 125 us
  waiting for transfers between devices  48.1 us (38%)
  starting transfers between devices  47.2 us (37%)
  Pallas kernels  15.9 us (13%)
  local copies, waits for them, and re-layouts  13.3 us (10%)
    ppermute x12, waiting for transfers between devices, send(): return lax.ppermute(x, AXES, pairs)  48.1 us
    ppermute x12, starting transfers between devices, send(): return lax.ppermute(x, AXES, pairs)  47.2 us
    pallas_call x3, Pallas kernels, call(): pl.pallas_call(kernel, out_shape=outs, in_specs=ins, out_specs=tuple((VME...  15.9 us
    unnamed x32, local copies, waits for them, and re-layouts  13.3 us
  transfers between devices with their start and end apart: 12, of which 4 were waited for; matrix products, arithmetic and copies ran while one was open for 0% of the time, Pallas kernels for 2%

profile of v1, /device:TPU:6, one launch (start us, length us, event | category | flops | bytes accessed | tf_op | source)
XLA Modules:
  0.0 125.4 jit_solution(7548371893246720149)
XLA Ops:
  0.6 0.0 copy-start
  0.6 1.2 copy-done
  1.9 1.2 copy-done.1
  3.1 0.7 copy-done.2
  3.8 3.3 %shard_map.50 = (bf16[784,128]{1,0:T(8,128)(2,1)S(1)}, bf16[1296,128]{1,0:T(8,128)(2,1)S(1)}, bf16[2432,128]{1,0:T(8,128)(2,1)S(1)}, bf16[1536,128]{1,0:T(8,128)...) custom-call(s32[4,8]{1,0:T(4,128)S(1)} %copy-done.2, ...), custom_call_target="tpu_custom_call" | custom-call | bytes 8003712 | tf_op jit(solution)/shard_map/pallas_call | solution.py:193
  7.0 13.5 %collective-permute-start.1 = (bf16[1296,128]{1,0:T(8,128)(2,1)S(1)}, bf16[1296,128]{1,0:T(8,128)(2,1)S(1)}, u32[]{:S(2)}, u32[]{:S(2)}) collective-permute-start(bf16[1296,128]{1,0:T(8,128)(2,1)S(1)} %get-tuple-element.16), channel_id=1, source_target_pairs={{1,0},{2,1},{3,2},{4,3},{5,4},{6,5},{7,6},{8,7},{9,8},{10,9},{11,1... | collective-permute-start | bytes 995336 | tf_op jit(solution)/shard_map/ppermute | solution.py:219
  20.6 1.5 %collective-permute-start.6 = (bf16[2432,128]{1,0:T(8,128)(2,1)S(1)}, bf16[2432,128]{1,0:T(8,128)(2,1)}, u32[]{:S(2)}, u32[]{:S(2)}) collective-permute-start(bf16[2432,128]{1,0:T(8,128)(2,1)S(1)} %get-tuple-element.20), channel_id=1, source_target_pairs={{7,15},{15,23},{23,31},{31,39},{39,47},{47,55},{55,63},{63,71},{71... | collective-permute-start | bytes 1867784 | tf_op jit(solution)/shard_map/ppermute | solution.py:219
  22.1 2.2 %collective-permute-start.8 = (bf16[2304,128]{1,0:T(8,128)(2,1)S(1)}, bf16[2304,128]{1,0:T(8,128)(2,1)}, u32[]{:S(2)}, u32[]{:S(2)}) collective-permute-start(bf16[2304,128]{1,0:T(8,128)(2,1)S(1)} %get-tuple-element.21), channel_id=1, source_target_pairs={{504,496},{496,488},{488,480},{480,472},{472,464},{464,456},{456,4... | collective-permute-start | bytes 1769480 | tf_op jit(solution)/shard_map/ppermute | solution.py:219
  24.2 1.9 %collective-permute-start = (bf16[784,128]{1,0:T(8,128)(2,1)S(1)}, bf16[784,128]{1,0:T(8,128)(2,1)S(1)}, u32[]{:S(2)}, u32[]{:S(2)}) collective-permute-start(bf16[784,128]{1,0:T(8,128)(2,1)S(1)} %get-tuple-element.15), channel_id=1, source_target_pairs={{0,1},{1,2},{2,3},{3,4},{4,5},{5,6},{6,7},{7,8},{8,9},{9,10},{10,1... | collective-permute-start | bytes 602120 | tf_op jit(solution)/shard_map/ppermute | solution.py:219
  26.2 8.8 %collective-permute-start.3 = (bf16[1536,128]{1,0:T(8,128)(2,1)S(1)}, bf16[1536,128]{1,0:T(8,128)(2,1)S(1)}, u32[]{:S(2)}, u32[]{:S(2)}) collective-permute-start(bf16[1536,128]{1,0:T(8,128)(2,1)S(1)} %get-tuple-element.19), channel_id=1, source_target_pairs={{1,0},{2,1},{3,2},{4,3},{5,4},{6,5},{7,6},{8,7},{9,8},{10,9},{11,1... | collective-permute-start | bytes 1179656 | tf_op jit(solution)/shard_map/ppermute | solution.py:219
  34.9 7.7 %collective-permute-done.r1 = bf16[784,128]{1,0:T(8,128)(2,1)S(1)} collective-permute-done((bf16[784,128]{1,0:T(8,128)(2,1)S(1)}, bf16[784,128]{1,0:T(8,128)(2,1)S(1)}, u32[]{:S(2)}, u32[]{:S(2)}) %collective-permute-start) | collective-permute-done | bytes 200736 | tf_op jit(solution)/shard_map/ppermute | solution.py:219
  42.6 1.3 %collective-permute-start.5 = (bf16[2304,128]{1,0:T(8,128)(2,1)S(1)}, bf16[2304,128]{1,0:T(8,128)(2,1)S(1)}, u32[]{:S(2)}, u32[]{:S(2)}) collective-permute-start(bf16[2304,128]{1,0:T(8,128)(2,1)S(1)} %get-tuple-element.21), channel_id=1, source_target_pairs={{1,0},{2,1},{3,2},{4,3},{5,4},{6,5},{7,6},{9,8},{10,9},{11,10},{12... | collective-permute-start | bytes 1769480 | tf_op jit(solution)/shard_map/ppermute | solution.py:219
  43.9 0.0 collective-permute-done.1.l1
  43.9 0.0 copy-start.8
  43.9 0.0 copy-start.4
  43.9 1.5 %copy-done.4 = bf16[512,1536]{1,0:T(8,128)(2,1)S(1)} copy-done((bf16[512,1536]{1,0:T(8,128)(2,1)S(1)}, bf16[512,1536]{1,0:T(8,128)(2,1)}, u32[]{:S(2)}) %copy-start.4) | copy-done | bytes 1572888
  45.4 1.4 %copy-done.5 = bf16[512,1536]{1,0:T(8,128)(2,1)S(1)} copy-done((bf16[512,1536]{1,0:T(8,128)(2,1)S(1)}, bf16[512,1536]{1,0:T(8,128)(2,1)}, u32[]{:S(2)}) %copy-start.5) | copy-done | bytes 1572888
  46.9 2.7 %shard_map.51 = (bf16[512,512]{1,0:T(8,128)(2,1)S(1)}, bf16[1280,128]{1,0:T(8,128)(2,1)}, bf16[768,128]{1,0:T(8,128)(2,1)S(1)}) custom-call(s32[4,8]{1,0:T(4,128)S(1)} %copy-done.2, bf16[512,1536]{1,0:T(8,128)(2,1)S(1)} %copy-done.4, bf16[512,1536]{1,0:T(8,128)(2,1)S(1)} %copy-done.5, bf16[784,128]{1,0:T(8,128)(2,1)S(1)} %collective-permute-done.r1, ...), custom_call_target="tpu_custom_call" | custom-call | flops 1342177280 | bytes 4726912 | tf_op jit(solution)/shard_map/pallas_call | solution.py:193
  49.6 0.0 copy-done.10
  49.6 0.0 copy-done.8
  49.6 0.8 copy-done.14
  50.4 1.9 %collective-permute-start.11 = (bf16[768,128]{1,0:T(8,128)(2,1)S(1)}, bf16[768,128]{1,0:T(8,128)(2,1)S(1)}, u32[]{:S(2)}, u32[]{:S(2)}) collective-permute-start(bf16[768,128]{1,0:T(8,128)(2,1)S(1)} %get-tuple-element.23), channel_id=1, source_target_pairs={{1,0},{2,1},{3,2},{4,3},{5,4},{6,5},{7,6},{8,7},{9,8},{10,9},{11,1... | collective-permute-start | bytes 589832 | tf_op jit(solution)/shard_map/ppermute | solution.py:219
  52.3 0.0 collective-permute-done.3.l2
  52.3 4.6 %collective-permute-start.2 = (bf16[2432,128]{1,0:T(8,128)(2,1)S(1)}, bf16[2432,128]{1,0:T(8,128)(2,1)S(1)}, u32[]{:S(2)}, u32[]{:S(2)}) collective-permute-start(bf16[2432,128]{1,0:T(8,128)(2,1)S(1)} %get-tuple-element.18), channel_id=1, source_target_pairs={{0,1},{1,2},{2,3},{3,4},{4,5},{5,6},{6,7},{7,8},{8,9},{9,10},{10,1... | collective-permute-start | bytes 1867784 | tf_op jit(solution)/shard_map/ppermute | solution.py:219
  56.8 3.9 %collective-permute-done.11.l = bf16[768,128]{1,0:T(8,128)(2,1)S(1)} collective-permute-done((bf16[768,128]{1,0:T(8,128)(2,1)S(1)}, bf16[768,128]{1,0:T(8,128)(2,1)S(1)}, u32[]{:S(2)}, u32[]{:S(2)}) %collective-permute-start.11) | collective-permute-done | bytes 196640 | tf_op jit(solution)/shard_map/ppermute | solution.py:219
  60.7 0.7 copy-done.12
  61.4 1.8 %collective-permute-start.4 = (bf16[2432,128]{1,0:T(8,128)(2,1)S(1)}, bf16[2432,128]{1,0:T(8,128)(2,1)S(1)}, u32[]{:S(2)}, u32[]{:S(2)}) collective-permute-start(bf16[2432,128]{1,0:T(8,128)(2,1)S(1)} %get-tuple-element.20), channel_id=1, source_target_pairs={{0,1},{1,2},{2,3},{3,4},{4,5},{5,6},{6,7},{8,9},{9,10},{10,11},{11... | collective-permute-start | bytes 1867784 | tf_op jit(solution)/shard_map/ppermute | solution.py:219
  63.2 0.0 collective-permute-done.6
  63.2 1.3 %collective-permute-start.7 = (bf16[2432,128]{1,0:T(8,128)(2,1)}, bf16[2432,128]{1,0:T(8,128)(2,1)S(1)}, u32[]{:S(2)}, u32[]{:S(2)}) collective-permute-start(bf16[2432,128]{1,0:T(8,128)(2,1)} %collective-permute-done.6), channel_id=1, source_target_pairs={{7,0},{15,8},{23,16},{31,24},{39,32},{47,40},{55,48},{63,56},{71,6... | collective-permute-start | bytes 1867784 | tf_op jit(solution)/shard_map/ppermute | solution.py:219
  64.5 0.0 collective-permute-done.8
  64.5 6.6 %collective-permute-start.9 = (bf16[2304,128]{1,0:T(8,128)(2,1)}, bf16[2304,128]{1,0:T(8,128)(2,1)}, u32[]{:S(2)}, u32[]{:S(2)}) collective-permute-start(bf16[2304,128]{1,0:T(8,128)(2,1)} %collective-permute-done.8), channel_id=1, source_target_pairs={{504,511},{496,503},{488,495},{480,487},{472,479},{464,471},{456,4... | collective-permute-start | bytes 1769480 | tf_op jit(solution)/shard_map/ppermute | solution.py:219
  71.1 0.0 collective-permute-done.5.l3
  71.1 0.8 copy-done.6
  71.9 1.9 %collective-permute-start.10 = (bf16[1280,128]{1,0:T(8,128)(2,1)}, bf16[1280,128]{1,0:T(8,128)(2,1)}, u32[]{:S(2)}, u32[]{:S(2)}) collective-permute-start(bf16[1280,128]{1,0:T(8,128)(2,1)} %get-tuple-element.22), channel_id=1, source_target_pairs={{0,1},{1,2},{2,3},{3,4},{4,5},{5,6},{6,7},{7,8},{8,9},{9,10},{10,1... | collective-permute-start | bytes 983048 | tf_op jit(solution)/shard_map/ppermute | solution.py:219
  73.9 0.1 add_convert_fusion.edge
  73.9 14.1 %collective-permute-done.2.r2 = bf16[2432,128]{1,0:T(8,128)(2,1)S(1)} collective-permute-done((bf16[2432,128]{1,0:T(8,128)(2,1)S(1)}, bf16[2432,128]{1,0:T(8,128)(2,1)S(1)}, u32[]{:S(2)}, u32[]{:S(2)}) %collective-permute-start.2) | collective-permute-done | bytes 622624 | tf_op jit(solution)/shard_map/ppermute | solution.py:219
  88.0 0.0 collective-permute-done.4.r3
  88.0 22.4 %collective-permute-done.10.e = bf16[1280,128]{1,0:T(8,128)(2,1)} collective-permute-done((bf16[1280,128]{1,0:T(8,128)(2,1)}, bf16[1280,128]{1,0:T(8,128)(2,1)}, u32[]{:S(2)}, u32[]{:S(2)}) %collective-permute-start.10) | collective-permute-done | bytes 327712 | tf_op jit(solution)/shard_map/ppermute | solution.py:219
  110.5 0.0 collective-permute-done.9.l3b
  110.5 0.0 collective-permute-done.7.r3b
  110.5 0.0 copy-done.3
  110.5 0.0 copy-start.7
  110.5 1.1 copy-done.7
  111.6 1.0 copy-done.9
  112.5 0.9 copy-done.11
  113.5 0.9 copy-done.13
  114.4 1.0 copy-done.15
  115.4 9.9 %shard_map.52 = (bf16[4,8,128,128]{3,2,1,0:T(8,128)(2,1)}, bf16[4,8,128,128]{3,2,1,0:T(8,128)(2,1)}) custom-call(s32[2]{0:T(128)S(1)} %add_convert_fusion.edge, s32[4,8]{1,0:T(4,128)S(1)} %copy-done.3, bf16[512,1536]{1,0:T(8,128)(2,1)} %get-tuple-element.13.yw, bf16[512,1536]{1,0:T(8,128)(2,1)} %get-tuple-element.14.zw, bf16[512,512]{1,0:T(8,128)(2,1)S(1)} %copy-done.15, ...), custom_call_target="tpu_custom_call" | custom-call | flops 5368709120 | bytes 10264712 | tf_op jit(solution)/shard_map/pallas_call | solution.py:193
  (12 shorter events, 0.0 us)
Async XLA Ops:
  0.6 1.2 copy-start
  1.9 1.2 copy-start.1
  3.1 0.7 copy-start.2
  7.0 36.9 %collective-permute-start.1 = (bf16[1296,128]{1,0:T(8,128)(2,1)S(1)}, bf16[1296,128]{1,0:T(8,128)(2,1)S(1)}, u32[]{:S(2)}, u32[]{:S(2)}) collective-permute-start(bf16[1296,128]{1,0:T(8,128)(2,1)S(1)} %get-tuple-element.16), channel_id=1, source_target_pairs={{1,0},{2,1},{3,2},{4,3},{5,4},{6,5},{7,6},{8,7},{9,8},{10,9},{11,1... | collective-permute-start | bytes 995336 | tf_op jit(solution)/shard_map/ppermute | solution.py:219
  20.6 42.6 %collective-permute-start.6 = (bf16[2432,128]{1,0:T(8,128)(2,1)S(1)}, bf16[2432,128]{1,0:T(8,128)(2,1)}, u32[]{:S(2)}, u32[]{:S(2)}) collective-permute-start(bf16[2432,128]{1,0:T(8,128)(2,1)S(1)} %get-tuple-element.20), channel_id=1, source_target_pairs={{7,15},{15,23},{23,31},{31,39},{39,47},{47,55},{55,63},{63,71},{71... | collective-permute-start | bytes 1867784 | tf_op jit(solution)/shard_map/ppermute | solution.py:219
  22.1 42.4 %collective-permute-start.8 = (bf16[2304,128]{1,0:T(8,128)(2,1)S(1)}, bf16[2304,128]{1,0:T(8,128)(2,1)}, u32[]{:S(2)}, u32[]{:S(2)}) collective-permute-start(bf16[2304,128]{1,0:T(8,128)(2,1)S(1)} %get-tuple-element.21), channel_id=1, source_target_pairs={{504,496},{496,488},{488,480},{480,472},{472,464},{464,456},{456,4... | collective-permute-start | bytes 1769480 | tf_op jit(solution)/shard_map/ppermute | solution.py:219
  24.2 18.4 %collective-permute-start = (bf16[784,128]{1,0:T(8,128)(2,1)S(1)}, bf16[784,128]{1,0:T(8,128)(2,1)S(1)}, u32[]{:S(2)}, u32[]{:S(2)}) collective-permute-start(bf16[784,128]{1,0:T(8,128)(2,1)S(1)} %get-tuple-element.15), channel_id=1, source_target_pairs={{0,1},{1,2},{2,3},{3,4},{4,5},{5,6},{6,7},{7,8},{8,9},{9,10},{10,1... | collective-permute-start | bytes 602120 | tf_op jit(solution)/shard_map/ppermute | solution.py:219
  26.2 26.1 %collective-permute-start.3 = (bf16[1536,128]{1,0:T(8,128)(2,1)S(1)}, bf16[1536,128]{1,0:T(8,128)(2,1)S(1)}, u32[]{:S(2)}, u32[]{:S(2)}) collective-permute-start(bf16[1536,128]{1,0:T(8,128)(2,1)S(1)} %get-tuple-element.19), channel_id=1, source_target_pairs={{1,0},{2,1},{3,2},{4,3},{5,4},{6,5},{7,6},{8,7},{9,8},{10,9},{11,1... | collective-permute-start | bytes 1179656 | tf_op jit(solution)/shard_map/ppermute | solution.py:219
  42.6 7.0 %copy-start.10 = (bf16[784,128]{1,0:T(8,128)(2,1)}, bf16[784,128]{1,0:T(8,128)(2,1)S(1)}, u32[]{:S(2)}) copy-start(bf16[784,128]{1,0:T(8,128)(2,1)S(1)} %collective-permute-done.r1) | copy-start | bytes 602116
  42.6 28.5 %collective-permute-start.5 = (bf16[2304,128]{1,0:T(8,128)(2,1)S(1)}, bf16[2304,128]{1,0:T(8,128)(2,1)S(1)}, u32[]{:S(2)}, u32[]{:S(2)}) collective-permute-start(bf16[2304,128]{1,0:T(8,128)(2,1)S(1)} %get-tuple-element.21), channel_id=1, source_target_pairs={{1,0},{2,1},{3,2},{4,3},{5,4},{6,5},{7,6},{9,8},{10,9},{11,10},{12... | collective-permute-start | bytes 1769480 | tf_op jit(solution)/shard_map/ppermute | solution.py:219
  43.9 5.7 %copy-start.8 = (bf16[1296,128]{1,0:T(8,128)(2,1)}, bf16[1296,128]{1,0:T(8,128)(2,1)S(1)}, u32[]{:S(2)}) copy-start(bf16[1296,128]{1,0:T(8,128)(2,1)S(1)} %collective-permute-done.1.l1) | copy-start | bytes 995332
  43.9 1.5 %copy-start.4 = (bf16[512,1536]{1,0:T(8,128)(2,1)S(1)}, bf16[512,1536]{1,0:T(8,128)(2,1)}, u32[]{:S(2)}) copy-start(bf16[512,1536]{1,0:T(8,128)(2,1)} %get-tuple-element.13.yw) | copy-start | bytes 4718596
  45.4 1.4 %copy-start.5 = (bf16[512,1536]{1,0:T(8,128)(2,1)S(1)}, bf16[512,1536]{1,0:T(8,128)(2,1)}, u32[]{:S(2)}) copy-start(bf16[512,1536]{1,0:T(8,128)(2,1)} %get-tuple-element.14.zw) | copy-start | bytes 4718596
  46.9 63.6 %copy-start.3 = (s32[4,8]{1,0:T(4,128)S(1)}, s32[4,8]{1,0:T(4,128)}, u32[]{:S(2)}) copy-start(s32[4,8]{1,0:T(4,128)} %pattern.5) | copy-start | bytes 388
  49.6 0.8 copy-start.14
  50.4 10.3 %collective-permute-start.11 = (bf16[768,128]{1,0:T(8,128)(2,1)S(1)}, bf16[768,128]{1,0:T(8,128)(2,1)S(1)}, u32[]{:S(2)}, u32[]{:S(2)}) collective-permute-start(bf16[768,128]{1,0:T(8,128)(2,1)S(1)} %get-tuple-element.23), channel_id=1, source_target_pairs={{1,0},{2,1},{3,2},{4,3},{5,4},{6,5},{7,6},{8,7},{9,8},{10,9},{11,1... | collective-permute-start | bytes 589832 | tf_op jit(solution)/shard_map/ppermute | solution.py:219
  52.3 35.8 %collective-permute-start.2 = (bf16[2432,128]{1,0:T(8,128)(2,1)S(1)}, bf16[2432,128]{1,0:T(8,128)(2,1)S(1)}, u32[]{:S(2)}, u32[]{:S(2)}) collective-permute-start(bf16[2432,128]{1,0:T(8,128)(2,1)S(1)} %get-tuple-element.18), channel_id=1, source_target_pairs={{0,1},{1,2},{2,3},{3,4},{4,5},{5,6},{6,7},{7,8},{8,9},{9,10},{10,1... | collective-permute-start | bytes 1867784 | tf_op jit(solution)/shard_map/ppermute | solution.py:219
  60.7 0.7 copy-start.12
  61.4 26.7 %collective-permute-start.4 = (bf16[2432,128]{1,0:T(8,128)(2,1)S(1)}, bf16[2432,128]{1,0:T(8,128)(2,1)S(1)}, u32[]{:S(2)}, u32[]{:S(2)}) collective-permute-start(bf16[2432,128]{1,0:T(8,128)(2,1)S(1)} %get-tuple-element.20), channel_id=1, source_target_pairs={{0,1},{1,2},{2,3},{3,4},{4,5},{5,6},{6,7},{8,9},{9,10},{10,11},{11... | collective-permute-start | bytes 1867784 | tf_op jit(solution)/shard_map/ppermute | solution.py:219
  63.2 47.3 %collective-permute-start.7 = (bf16[2432,128]{1,0:T(8,128)(2,1)}, bf16[2432,128]{1,0:T(8,128)(2,1)S(1)}, u32[]{:S(2)}, u32[]{:S(2)}) collective-permute-start(bf16[2432,128]{1,0:T(8,128)(2,1)} %collective-permute-done.6), channel_id=1, source_target_pairs={{7,0},{15,8},{23,16},{31,24},{39,32},{47,40},{55,48},{63,56},{71,6... | collective-permute-start | bytes 1867784 | tf_op jit(solution)/shard_map/ppermute | solution.py:219
  64.5 46.0 %collective-permute-start.9 = (bf16[2304,128]{1,0:T(8,128)(2,1)}, bf16[2304,128]{1,0:T(8,128)(2,1)}, u32[]{:S(2)}, u32[]{:S(2)}) collective-permute-start(bf16[2304,128]{1,0:T(8,128)(2,1)} %collective-permute-done.8), channel_id=1, source_target_pairs={{504,511},{496,503},{488,495},{480,487},{472,479},{464,471},{456,4... | collective-permute-start | bytes 1769480 | tf_op jit(solution)/shard_map/ppermute | solution.py:219
  71.1 0.8 copy-start.6
  71.9 38.5 %collective-permute-start.10 = (bf16[1280,128]{1,0:T(8,128)(2,1)}, bf16[1280,128]{1,0:T(8,128)(2,1)}, u32[]{:S(2)}, u32[]{:S(2)}) collective-permute-start(bf16[1280,128]{1,0:T(8,128)(2,1)} %get-tuple-element.22), channel_id=1, source_target_pairs={{0,1},{1,2},{2,3},{3,4},{4,5},{5,6},{6,7},{7,8},{8,9},{9,10},{10,1... | collective-permute-start | bytes 983048 | tf_op jit(solution)/shard_map/ppermute | solution.py:219
  110.5 1.1 copy-start.7
  111.6 1.0 copy-start.9
  112.5 0.9 copy-start.11
  113.5 0.9 copy-start.13
  114.4 1.0 copy-start.15

commit v2 on v1

v2 whole, which is shorter than its diff:
```python
import jax
import jax.numpy as jnp
from jax import lax
from jax.experimental import pallas as pl
from jax.experimental.pallas import tpu as pltpu
from jax.sharding import PartitionSpec as P

AXES = ("row", "col")
B = 128
S = 512
H = 256
RING = 8
BF = jnp.bfloat16
F32 = jnp.float32

LOWER = [(r, c) for r in range(4) for c in range(r, 4)]
UPPER = [(r, c) for r in range(4) for c in range(r)]
FULL = [(r, c) for r in range(4) for c in range(4)]


def of(name, blocks):
    return [(name, r, c) for r, c in blocks]


R1 = of("yU", UPPER)
L1 = of("yL", LOWER)
L_TOP = [p for p in LOWER if p[0] < 3]
R_REST = of("yD", FULL) + of("zU", UPPER) + of("zD", FULL)
L_REST = of("yD", [(r, c) for r in range(3) for c in range(3)]) + of("zL", L_TOP) + of("zD", FULL[:12])
R2, R3 = R_REST[:18], R_REST[18:]
L2, L3 = L_REST[:13], L_REST[13:]
COLUMN = {"L": 0, "D": S, "U": 2 * S}
QUADS = {
    "L": ((0, 0), (0, 1), (1, 1)),
    "D": ((0, 0), (0, 1), (1, 0), (1, 1)),
    "U": ((0, 0), (1, 0), (1, 1)),
}
BLOCKS = {"L": LOWER, "D": FULL, "U": UPPER}


def slot(part, r, c):
    return c - r + {"L": 0, "D": 4, "U": 8}[part]


def rows(i, n=1):
    return pl.ds(i * B, n * B)


def unpack(message, ref, into):
    for i, (name, r, c) in enumerate(message):
        target, column = into[name]
        target[rows(r), pl.ds(column + c * B, B)] = ref[rows(i), :]


def clear(target, column, blocks):
    for r, c in FULL:
        if (r, c) not in blocks:
            target[rows(r), pl.ds(column + c * B, B)] = jnp.zeros((B, B), target.dtype)


def product(acc, part, *terms):
    for i, n in QUADS[part]:
        total = None
        for (left, lc, lp), (right, rc, rp) in terms:
            ks = [k for k in (0, 1) if (i, k) in QUADS[lp] and (k, n) in QUADS[rp]]
            if not ks:
                continue
            low, size = ks[0] * H, len(ks) * H
            value = jnp.dot(
                left[pl.ds(i * H, H), pl.ds(lc + low, size)],
                right[pl.ds(low, size), pl.ds(rc + n * H, H)],
                preferred_element_type=F32,
            )
            total = value if total is None else total + value
        acc[pl.ds(i * H, H), pl.ds(n * H, H)] = total


def side(ref, part, column=None):
    return ref, COLUMN[part] if column is None else column, part


def keep(pattern, part, r, c):
    d = slot(part, r, c)
    return True if d == 4 else pattern[r, d] == 1


def masked(flag, block):
    return block if flag is True else jnp.where(flag, block, jnp.zeros_like(block))


def pack_kernel(edge, pattern, y, z, r1, l1, r2, l2, r3, l3, zz, yw, zw, yin, zin, sems):
    copies = []
    for i, (source, target) in enumerate(((y, yin), (z, zin))):
        for r in range(4):
            copies.append(pltpu.make_async_copy(source.at[r], target.at[r], sems.at[i * 4 + r]))
            copies[-1].start()
    for copy in copies:
        copy.wait()
    for wide, source in ((yw, yin), (zw, zin)):
        for r in range(4):
            for d in range(8):
                k = True if d == 4 else pattern[r, d] == 1
                wide[rows(r), rows(r + d)] = masked(k, source[r, d])
            for c in range(12):
                if not r <= c < r + 8:
                    wide[rows(r), rows(c)] = jnp.zeros((B, B), BF)

    def fill(message, ref):
        for i, (name, r, c) in enumerate(message):
            wide = yw if name[0] == "y" else zw
            ref[rows(i), :] = wide[rows(r), pl.ds(COLUMN[name[1]] + c * B, B)]

    for message, ref in ((R1, r1), (L1, l1), (R2, r2), (L2, l2), (R3, r3), (L3, l3)):
        fill(message, ref)

    @pl.when(edge[0] == 1)
    def _():
        fill(L3, zz)

    @pl.when(edge[0] == 0)
    def _():
        fill(R3, zz)

    line = lax.broadcasted_iota(jnp.int32, (16, B), 0)
    for message, ref in ((R1, r1), (L1, l1)):
        tile = jnp.zeros((16, B), F32)
        for i, (name, r, c) in enumerate(message):
            k = keep(pattern, name[1], r, c)
            tile = jnp.where(line == i, 1.0 if k is True else jnp.where(k, 1.0, 0.0), tile)
        ref[pl.ds(len(message) * B, 16), :] = tile.astype(BF)


def middle_kernel(pattern, yw, zw, r1, l1, td, e, l, yu, yl, acc):
    clear(yu, 0, UPPER)
    clear(yl, 0, LOWER)
    unpack(R1, r1, {"yU": (yu, 0)})
    unpack(L1, l1, {"yL": (yl, 0)})
    product(
        acc,
        "D",
        (side(zw, "L"), side(yu, "U", 0)),
        (side(zw, "D"), side(yw, "D")),
        (side(zw, "U"), side(yl, "L", 0)),
    )
    eye = jnp.where(
        lax.broadcasted_iota(jnp.int32, (B, B), 0) == lax.broadcasted_iota(jnp.int32, (B, B), 1), 1.5, 0.0
    )
    for r, c in FULL:
        block = -0.5 * acc[rows(r), rows(c)]
        if r == c:
            block = block + eye
        td[rows(r), rows(c)] = masked(keep(pattern, "D", r, c), block).astype(BF)
    for part, left, out in (("L", yl, e), ("U", yu, l)):
        product(acc, part, (side(left, part, 0), side(td, "D", 0)))
        for i, (r, c) in enumerate(BLOCKS[part]):
            out[rows(i), :] = acc[rows(r), rows(c)].astype(BF)


def last_kernel(pattern, yw, zw, td, r1, l1, r2, l2, r3, l3, e, l, yout, zout, *scratch):
    ya, yc, za, zc, tw, tua, tlc, acc, yo, zo, sems = scratch
    for big in (ya, za):
        clear(big, S, UPPER)
    clear(yc, 0, LOWER)
    clear(zc, 0, L_TOP)
    clear(yc, S, [(r, c) for r in range(3) for c in range(3)])
    clear(zc, S, FULL[:12])
    left = {"yD": (ya, 0), "yU": (ya, S), "zD": (za, 0), "zU": (za, S)}
    right = {"yL": (yc, 0), "yD": (yc, S), "zL": (zc, 0), "zD": (zc, S)}
    for message, ref in ((R1, r1), (R2, r2), (R3, r3)):
        unpack(message, ref, left)
    for message, ref in ((L1, l1), (L2, l2), (L3, l3)):
        unpack(message, ref, right)
    clear(tw, COLUMN["L"], LOWER)
    clear(tw, COLUMN["U"], UPPER)
    clear(tua, 0, UPPER)
    clear(tlc, 0, L_TOP)
    product(acc, "L", (side(zw, "L"), side(ya, "D", 0)), (side(zw, "D"), side(yw, "L")))
    for r, c in LOWER:
        tw[rows(r), rows(c)] = masked(keep(pattern, "L", r, c), -0.5 * acc[rows(r), rows(c)]).astype(BF)
    product(acc, "U", (side(zw, "D"), side(yw, "U")), (side(zw, "U"), side(yc, "D", S)))
    for r, c in UPPER:
        tw[rows(r), pl.ds(2 * S + c * B, B)] = masked(
            keep(pattern, "U", r, c), -0.5 * acc[rows(r), rows(c)]
        ).astype(BF)
    left_mask = r1[pl.ds(len(R1) * B, 16), :].astype(F32)
    right_mask = l1[pl.ds(len(L1) * B, 16), :].astype(F32)
    product(acc, "U", (side(za, "D", 0), side(ya, "U", S)), (side(za, "U", S), side(yw, "D")))
    for i, (r, c) in enumerate(UPPER):
        tua[rows(r), rows(c)] = (-0.5 * acc[rows(r), rows(c)] * left_mask[i : i + 1, :]).astype(BF)
    product(acc, "L", (side(zc, "L", 0), side(yw, "D")), (side(zc, "D", S), side(yc, "L", 0)))
    for i, (r, c) in enumerate(LOWER):
        if r < 3:
            tlc[rows(r), rows(c)] = (-0.5 * acc[rows(r), rows(c)] * right_mask[i : i + 1, :]).astype(BF)

    t_l, t_u, t_d = side(tw, "L"), side(tw, "U"), side(td, "D", 0)

    def finish(out, part, *terms, extra=None):
        product(acc, part, *terms)
        for i, (r, c) in enumerate(BLOCKS[part]):
            block = acc[rows(r), rows(c)]
            if extra is not None:
                block = block + extra[rows(i), :].astype(F32)
            out[r, slot(part, r, c)] = masked(keep(pattern, part, r, c), block).astype(BF)

    copies = []

    def write(source, target):
        for r in range(4):
            copies.append(pltpu.make_async_copy(source.at[r], target.at[r], sems.at[len(copies)]))
            copies[-1].start()

    finish(zo, "L", (t_l, side(za, "D", 0)), (t_d, side(zw, "L")))
    finish(zo, "D", (t_l, side(za, "U", S)), (t_d, side(zw, "D")), (t_u, side(zc, "L", 0)))
    finish(zo, "U", (t_d, side(zw, "U")), (t_u, side(zc, "D", S)))
    write(zo, zout)
    finish(
        yo, "D", (side(yw, "L"), side(tua, "U", 0)), (side(yw, "D"), t_d), (side(yw, "U"), side(tlc, "L", 0))
    )
    finish(yo, "L", (side(yw, "D"), t_l), extra=e)
    finish(yo, "U", (side(yw, "D"), t_u), extra=l)
    write(yo, yout)
    for copy in copies:
        copy.wait()


VMEM = pl.BlockSpec(memory_space=pltpu.VMEM)
SMEM = pl.BlockSpec(memory_space=pltpu.SMEM)
ANY = pl.BlockSpec(memory_space=pl.ANY)


def packed(blocks, masks=False):
    return jax.ShapeDtypeStruct((len(blocks) * B + 16 * masks, B), BF)


def call(kernel, outs, out_specs, ins, scratch, flops, operands):
    outs = tuple(outs)
    moved = sum(v.size * v.dtype.itemsize for v in (*outs, *operands))
    return pl.pallas_call(
        kernel,
        out_shape=outs,
        in_specs=ins,
        out_specs=tuple(out_specs),
        scratch_shapes=scratch,
        compiler_params=pltpu.CompilerParams(vmem_limit_bytes=VMEM_LIMIT),
        cost_estimate=pl.CostEstimate(flops=flops, bytes_accessed=moved, transcendentals=0),
    )(*operands)


VMEM_LIMIT = 32 * 2**20


def local(ymatrix, zmatrix, pattern):
    count = lax.axis_size("row") * lax.axis_size("col")
    place = lax.axis_index("col") % RING
    first, last = place == 0, place == RING - 1
    right = [(i, (i + 1) % count) for i in range(count)]
    left = [(b, a) for a, b in right]
    ends = [(i, (i + RING) % count) for i in range(count) if i % RING == RING - 1]
    ends += [((i + RING) % count, i) for i in range(count) if i % RING == 0]
    right_y = [(i, i + 1 if i % RING < RING - 1 else i - RING + 1) for i in range(count)]
    left_y = [(b, a) for a, b in right_y]

    def send(x, pairs):
        return lax.ppermute(x, AXES, pairs)

    wide = jax.ShapeDtypeStruct((S, 3 * S), BF)
    edge = jnp.stack([first, last]).astype(jnp.int32)
    r1, l1, r2, l2, r3, l3, zz, yw, zw = call(
        pack_kernel,
        (packed(R1, True), packed(L1, True)) + tuple(packed(m) for m in (R2, L2, R3, L3, R3)) + (wide, wide),
        [VMEM] * 9,
        [SMEM, SMEM, ANY, ANY],
        [
            pltpu.VMEM(ymatrix.shape, BF),
            pltpu.VMEM(ymatrix.shape, BF),
            pltpu.SemaphoreType.DMA((8,)),
        ],
        0,
        (edge, pattern, ymatrix, zmatrix),
    )
    r1, l1 = send(r1, right), send(l1, left)
    zz = send(zz, ends)
    r2, l2 = send(r2, right), send(l2, left)
    td, e, l = call(
        middle_kernel,
        (jax.ShapeDtypeStruct((S, S), BF), packed(LOWER), packed(UPPER)),
        [VMEM] * 3,
        [SMEM] + [VMEM] * 4,
        [pltpu.VMEM((S, S), BF), pltpu.VMEM((S, S), BF), pltpu.VMEM((S, S), F32)],
        6 * S**3,
        (pattern, yw, zw, r1, l1),
    )
    e, l = send(e, right), send(l, left)
    r3 = send(jnp.where(last, zz, r3), right_y)
    l3 = send(jnp.where(first, zz[: len(L3) * B], l3), left_y)
    whole = jax.ShapeDtypeStruct(ymatrix.shape, BF)
    half = pltpu.VMEM((S, 2 * S), BF)
    return call(
        last_kernel,
        (whole, whole),
        [ANY] * 2,
        [SMEM] + [VMEM] * 11,
        [
            half,
            half,
            half,
            half,
            pltpu.VMEM((S, 3 * S), BF),
            pltpu.VMEM((S, S), BF),
            pltpu.VMEM((S, S), BF),
            pltpu.VMEM((S, S), F32),
            pltpu.VMEM(ymatrix.shape, BF),
            pltpu.VMEM(ymatrix.shape, BF),
            pltpu.SemaphoreType.DMA((8,)),
        ],
        20 * S**3,
        (pattern, yw, zw, td, r1, l1, r2, l2, r3, l3, e, l),
    )


def solution(mesh):
    band = P(AXES, None, None, None)
    return jax.shard_map(
        local,
        mesh=mesh,
        in_specs=(band, band, P(AXES, None)),
        out_specs=(band, band),
        check_vma=False,
    )
```

time: 127 us -> 93.6 us (0.74)
  waiting for transfers between devices: 48.1 us -> 32.8 us
  local copies, waits for them, and re-layouts: 13.3 us -> 3.13 us
  Pallas kernels: 15.9 us -> 9.92 us
    ppermute x12 -> x9, waiting for transfers between devices: 48.1 us -> 32.8 us  [send(): return lax.ppermute(x, AXES, pairs)]
    unnamed x32 -> x8, local copies, waits for them, and re-layouts: 13.3 us -> 3.13 us
    pallas_call x3, Pallas kernels: 15.9 us -> 9.92 us  [call(): pl.pallas_call(kernel, out_shape=outs, in_specs=ins, out_specs=tuple(out_...]
    ppermute x12 -> x9, starting transfers between devices: 47.2 us -> 46.3 us  [send(): return lax.ppermute(x, AXES, pairs)]
  transfers between devices with their start and end apart: 12 -> 9, of which waited for: 4 -> 3; matrix products, arithmetic and copies ran while one was open for 0% -> 0% of each run, Pallas kernels for 2% -> 2%
where the time goes in v2:
time: 93.6 us; the launch traced here: 93.1 us
  starting transfers between devices  46.3 us (49%)
  waiting for transfers between devices  32.8 us (35%)
  Pallas kernels  9.92 us (11%)
  local copies, waits for them, and re-layouts  3.13 us (3%)
    ppermute x9, starting transfers between devices, send(): return lax.ppermute(x, AXES, pairs)  46.3 us
    ppermute x9, waiting for transfers between devices, send(): return lax.ppermute(x, AXES, pairs)  32.8 us
    pallas_call x3, Pallas kernels, call(): pl.pallas_call(kernel, out_shape=outs, in_specs=ins, out_specs=tuple(out_...  9.92 us
    unnamed x8, local copies, waits for them, and re-layouts  3.13 us
  transfers between devices with their start and end apart: 9, of which 3 were waited for; matrix products, arithmetic and copies ran while one was open for 0% of the time, Pallas kernels for 2%

profile of v2, /device:TPU:6, one launch (start us, length us, event | category | flops | bytes accessed | tf_op | source)
XLA Modules:
  0.0 93.1 jit_solution(1956081537325233242)
XLA Ops:
  0.6 0.1 add_convert_fusion.edge
  0.7 0.0 copy-start
  0.7 1.2 %copy-done = bf16[4,8,128,128]{3,2,1,0:T(8,128)(2,1)S(1)} copy-done((bf16[4,8,128,128]{3,2,1,0:T(8,128)(2,1)S(1)}, bf16[4,8,128,128]{3,2,1,0:T(8,128)(2,1)}, u32[]{:S(2)}) %copy-start) | copy-done | bytes 1048600
  1.9 0.0 copy-start.1
  1.9 1.2 %copy-done.1 = bf16[4,8,128,128]{3,2,1,0:T(8,128)(2,1)S(1)} copy-done((bf16[4,8,128,128]{3,2,1,0:T(8,128)(2,1)S(1)}, bf16[4,8,128,128]{3,2,1,0:T(8,128)(2,1)}, u32[]{:S(2)}) %copy-start.1) | copy-done | bytes 1048600
  3.2 0.0 copy-start.2
  3.2 0.7 copy-done.2
  3.9 2.0 %shard_map.50 = (bf16[784,128]{1,0:T(8,128)(2,1)S(1)}, bf16[1296,128]{1,0:T(8,128)(2,1)S(1)}, bf16[2304,128]{1,0:T(8,128)(2,1)S(1)}, bf16[1664,128]{1,0:T(8,128)...) custom-call(s32[2]{0:T(128)S(1)} %add_convert_fusion.edge, ...), custom_call_target="tpu_custom_call" | custom-call | bytes 8659080 | tf_op jit(solution)/shard_map/pallas_call | solution.py:238
  5.8 10.6 %collective-permute-start.4 = (bf16[2560,128]{1,0:T(8,128)(2,1)S(1)}, bf16[2560,128]{1,0:T(8,128)(2,1)S(1)}, u32[]{:S(2)}, u32[]{:S(2)}) collective-permute-start(bf16[2560,128]{1,0:T(8,128)(2,1)S(1)} %get-tuple-element.21), channel_id=1, source_target_pairs={{7,15},{15,23},{23,31},{31,39},{39,47},{47,55},{55,63},{63,71},{71... | collective-permute-start | bytes 1966088 | tf_op jit(solution)/shard_map/ppermute | solution.py:264
  16.5 1.9 %collective-permute-start = (bf16[784,128]{1,0:T(8,128)(2,1)S(1)}, bf16[784,128]{1,0:T(8,128)(2,1)S(1)}, u32[]{:S(2)}, u32[]{:S(2)}) collective-permute-start(bf16[784,128]{1,0:T(8,128)(2,1)S(1)} %get-tuple-element.16), channel_id=1, source_target_pairs={{0,1},{1,2},{2,3},{3,4},{4,5},{5,6},{6,7},{7,8},{8,9},{9,10},{10,1... | collective-permute-start | bytes 602120 | tf_op jit(solution)/shard_map/ppermute | solution.py:264
  18.4 8.8 %collective-permute-start.1 = (bf16[1296,128]{1,0:T(8,128)(2,1)S(1)}, bf16[1296,128]{1,0:T(8,128)(2,1)S(1)}, u32[]{:S(2)}, u32[]{:S(2)}) collective-permute-start(bf16[1296,128]{1,0:T(8,128)(2,1)S(1)} %get-tuple-element.17), channel_id=1, source_target_pairs={{1,0},{2,1},{3,2},{4,3},{5,4},{6,5},{7,6},{8,7},{9,8},{10,9},{11,1... | collective-permute-start | bytes 995336 | tf_op jit(solution)/shard_map/ppermute | solution.py:264
  27.2 1.9 %collective-permute-start.3 = (bf16[1664,128]{1,0:T(8,128)(2,1)S(1)}, bf16[1664,128]{1,0:T(8,128)(2,1)S(1)}, u32[]{:S(2)}, u32[]{:S(2)}) collective-permute-start(bf16[1664,128]{1,0:T(8,128)(2,1)S(1)} %get-tuple-element.20), channel_id=1, source_target_pairs={{1,0},{2,1},{3,2},{4,3},{5,4},{6,5},{7,6},{8,7},{9,8},{10,9},{11,1... | collective-permute-start | bytes 1277960 | tf_op jit(solution)/shard_map/ppermute | solution.py:264
  29.1 3.9 %collective-permute-start.2 = (bf16[2304,128]{1,0:T(8,128)(2,1)S(1)}, bf16[2304,128]{1,0:T(8,128)(2,1)S(1)}, u32[]{:S(2)}, u32[]{:S(2)}) collective-permute-start(bf16[2304,128]{1,0:T(8,128)(2,1)S(1)} %get-tuple-element.19), channel_id=1, source_target_pairs={{0,1},{1,2},{2,3},{3,4},{4,5},{5,6},{6,7},{7,8},{8,9},{9,10},{10,1... | collective-permute-start | bytes 1769480 | tf_op jit(solution)/shard_map/ppermute | solution.py:264
  33.0 12.4 %collective-permute-done.4 = bf16[2560,128]{1,0:T(8,128)(2,1)S(1)} collective-permute-done((bf16[2560,128]{1,0:T(8,128)(2,1)S(1)}, bf16[2560,128]{1,0:T(8,128)(2,1)S(1)}, u32[]{:S(2)}, u32[]{:S(2)}) %collective-permute-start.4) | collective-permute-done | bytes 655392 | tf_op jit(solution)/shard_map/ppermute | solution.py:264
  45.4 0.0 copy-start.3
  45.4 0.1 broadcast_select_fusion
  45.5 1.9 %collective-permute-start.5 = (bf16[2560,128]{1,0:T(8,128)(2,1)S(1)}, bf16[2560,128]{1,0:T(8,128)(2,1)S(1)}, u32[]{:S(2)}, u32[]{:S(2)}) collective-permute-start(bf16[2560,128]{1,0:T(8,128)(2,1)S(1)} %broadcast_select_fusion), channel_id=1, source_target_pairs={{0,1},{1,2},{2,3},{3,4},{4,5},{5,6},{6,7},{7,0},{8,9},{9,10},{10,1... | collective-permute-start | bytes 1966088 | tf_op jit(solution)/shard_map/ppermute | solution.py:264
  47.4 0.1 slice_select_fusion
  47.5 0.0 collective-permute-done.r1
  47.5 5.1 %collective-permute-start.6 = (bf16[2176,128]{1,0:T(8,128)(2,1)S(1)}, bf16[2176,128]{1,0:T(8,128)(2,1)S(1)}, u32[]{:S(2)}, u32[]{:S(2)}) collective-permute-start(bf16[2176,128]{1,0:T(8,128)(2,1)S(1)} %slice_select_fusion), channel_id=1, source_target_pairs={{1,0},{2,1},{3,2},{4,3},{5,4},{6,5},{7,6},{0,7},{9,8},{10,9},{11,1... | collective-permute-start | bytes 1671176 | tf_op jit(solution)/shard_map/ppermute | solution.py:264
  52.6 0.0 collective-permute-done.1.l1
  52.6 0.0 copy-done.3
  52.6 1.9 %shard_map.51 = (bf16[512,512]{1,0:T(8,128)(2,1)S(1)}, bf16[1280,128]{1,0:T(8,128)(2,1)S(1)}, bf16[768,128]{1,0:T(8,128)(2,1)S(1)}) custom-call(s32[4,8]{1,0:T(4,128)S(1)} %copy-done.3, bf16[512,1536]{1,0:T(8,128)(2,1)S(1)} %get-tuple-element.14.yw, bf16[512,1536]{1,0:T(8,128)(2,1)S(1)} %get-tuple-element.15.zw, ...), custom_call_target="tpu_custom_call" | custom-call | flops 805306368 | bytes 4726912 | tf_op jit(solution)/shard_map/pallas_call | solution.py:238
  54.5 1.9 %collective-permute-start.7 = (bf16[1280,128]{1,0:T(8,128)(2,1)S(1)}, bf16[1280,128]{1,0:T(8,128)(2,1)S(1)}, u32[]{:S(2)}, u32[]{:S(2)}) collective-permute-start(bf16[1280,128]{1,0:T(8,128)(2,1)S(1)} %get-tuple-element.24), channel_id=1, source_target_pairs={{0,1},{1,2},{2,3},{3,4},{4,5},{5,6},{6,7},{7,8},{8,9},{9,10},{10,1... | collective-permute-start | bytes 983048 | tf_op jit(solution)/shard_map/ppermute | solution.py:264
  56.5 0.0 collective-permute-done.3.l2
  56.5 10.1 %collective-permute-start.8 = (bf16[768,128]{1,0:T(8,128)(2,1)S(1)}, bf16[768,128]{1,0:T(8,128)(2,1)S(1)}, u32[]{:S(2)}, u32[]{:S(2)}) collective-permute-start(bf16[768,128]{1,0:T(8,128)(2,1)S(1)} %get-tuple-element.25), channel_id=1, source_target_pairs={{1,0},{2,1},{3,2},{4,3},{5,4},{6,5},{7,6},{8,7},{9,8},{10,9},{11,1... | collective-permute-start | bytes 589832 | tf_op jit(solution)/shard_map/ppermute | solution.py:264
  66.6 4.1 %collective-permute-done.8.l = bf16[768,128]{1,0:T(8,128)(2,1)S(1)} collective-permute-done((bf16[768,128]{1,0:T(8,128)(2,1)S(1)}, bf16[768,128]{1,0:T(8,128)(2,1)S(1)}, u32[]{:S(2)}, u32[]{:S(2)}) %collective-permute-start.8) | collective-permute-done | bytes 196640 | tf_op jit(solution)/shard_map/ppermute | solution.py:264
  70.7 0.0 collective-permute-done.2.r2
  70.7 16.3 %collective-permute-done.7.e = bf16[1280,128]{1,0:T(8,128)(2,1)S(1)} collective-permute-done((bf16[1280,128]{1,0:T(8,128)(2,1)S(1)}, bf16[1280,128]{1,0:T(8,128)(2,1)S(1)}, u32[]{:S(2)}, u32[]{:S(2)}) %collective-permute-start.7) | collective-permute-done | bytes 327712 | tf_op jit(solution)/shard_map/ppermute | solution.py:264
  87.0 0.0 collective-permute-done.6.l3
  87.0 0.0 collective-permute-done.5.r3
  87.0 6.1 %shard_map.52 = (bf16[4,8,128,128]{3,2,1,0:T(8,128)(2,1)}, bf16[4,8,128,128]{3,2,1,0:T(8,128)(2,1)}) custom-call(s32[4,8]{1,0:T(4,128)S(1)} %copy-done.3, bf16[512,1536]{1,0:T(8,128)(2,1)S(1)} %get-tuple-element.14.yw, bf16[512,1536]{1,0:T(8,128)(2,1)S(1)} %get-tuple-element.15.zw, bf16[512,512]{1,0:T(8,128)(2,1)S(1)} %get-tuple-element.18.td, ...), custom_call_target="tpu_custom_call" | custom-call | flops 2684354560 | bytes 9052288 | tf_op jit(solution)/shard_map/pallas_call | solution.py:238
Async XLA Ops:
  0.7 1.2 %copy-start = (bf16[4,8,128,128]{3,2,1,0:T(8,128)(2,1)S(1)}, bf16[4,8,128,128]{3,2,1,0:T(8,128)(2,1)}, u32[]{:S(2)}) copy-start(bf16[4,8,128,128]{3,2,1,0:T(8,128)(2,1)} %y.1) | copy-start | bytes 3145732
  1.9 1.2 %copy-start.1 = (bf16[4,8,128,128]{3,2,1,0:T(8,128)(2,1)S(1)}, bf16[4,8,128,128]{3,2,1,0:T(8,128)(2,1)}, u32[]{:S(2)}) copy-start(bf16[4,8,128,128]{3,2,1,0:T(8,128)(2,1)} %z.1) | copy-start | bytes 3145732
  3.2 0.7 copy-start.2
  5.8 39.6 %collective-permute-start.4 = (bf16[2560,128]{1,0:T(8,128)(2,1)S(1)}, bf16[2560,128]{1,0:T(8,128)(2,1)S(1)}, u32[]{:S(2)}, u32[]{:S(2)}) collective-permute-start(bf16[2560,128]{1,0:T(8,128)(2,1)S(1)} %get-tuple-element.21), channel_id=1, source_target_pairs={{7,15},{15,23},{23,31},{31,39},{39,47},{47,55},{55,63},{63,71},{71... | collective-permute-start | bytes 1966088 | tf_op jit(solution)/shard_map/ppermute | solution.py:264
  16.5 31.0 %collective-permute-start = (bf16[784,128]{1,0:T(8,128)(2,1)S(1)}, bf16[784,128]{1,0:T(8,128)(2,1)S(1)}, u32[]{:S(2)}, u32[]{:S(2)}) collective-permute-start(bf16[784,128]{1,0:T(8,128)(2,1)S(1)} %get-tuple-element.16), channel_id=1, source_target_pairs={{0,1},{1,2},{2,3},{3,4},{4,5},{5,6},{6,7},{7,8},{8,9},{9,10},{10,1... | collective-permute-start | bytes 602120 | tf_op jit(solution)/shard_map/ppermute | solution.py:264
  18.4 34.2 %collective-permute-start.1 = (bf16[1296,128]{1,0:T(8,128)(2,1)S(1)}, bf16[1296,128]{1,0:T(8,128)(2,1)S(1)}, u32[]{:S(2)}, u32[]{:S(2)}) collective-permute-start(bf16[1296,128]{1,0:T(8,128)(2,1)S(1)} %get-tuple-element.17), channel_id=1, source_target_pairs={{1,0},{2,1},{3,2},{4,3},{5,4},{6,5},{7,6},{8,7},{9,8},{10,9},{11,1... | collective-permute-start | bytes 995336 | tf_op jit(solution)/shard_map/ppermute | solution.py:264
  27.2 29.3 %collective-permute-start.3 = (bf16[1664,128]{1,0:T(8,128)(2,1)S(1)}, bf16[1664,128]{1,0:T(8,128)(2,1)S(1)}, u32[]{:S(2)}, u32[]{:S(2)}) collective-permute-start(bf16[1664,128]{1,0:T(8,128)(2,1)S(1)} %get-tuple-element.20), channel_id=1, source_target_pairs={{1,0},{2,1},{3,2},{4,3},{5,4},{6,5},{7,6},{8,7},{9,8},{10,9},{11,1... | collective-permute-start | bytes 1277960 | tf_op jit(solution)/shard_map/ppermute | solution.py:264
  29.1 41.6 %collective-permute-start.2 = (bf16[2304,128]{1,0:T(8,128)(2,1)S(1)}, bf16[2304,128]{1,0:T(8,128)(2,1)S(1)}, u32[]{:S(2)}, u32[]{:S(2)}) collective-permute-start(bf16[2304,128]{1,0:T(8,128)(2,1)S(1)} %get-tuple-element.19), channel_id=1, source_target_pairs={{0,1},{1,2},{2,3},{3,4},{4,5},{5,6},{6,7},{7,8},{8,9},{9,10},{10,1... | collective-permute-start | bytes 1769480 | tf_op jit(solution)/shard_map/ppermute | solution.py:264
  45.4 7.2 %copy-start.3 = (s32[4,8]{1,0:T(4,128)S(1)}, s32[4,8]{1,0:T(4,128)}, u32[]{:S(2)}) copy-start(s32[4,8]{1,0:T(4,128)} %pattern.5) | copy-start | bytes 388
  45.5 41.6 %collective-permute-start.5 = (bf16[2560,128]{1,0:T(8,128)(2,1)S(1)}, bf16[2560,128]{1,0:T(8,128)(2,1)S(1)}, u32[]{:S(2)}, u32[]{:S(2)}) collective-permute-start(bf16[2560,128]{1,0:T(8,128)(2,1)S(1)} %broadcast_select_fusion), channel_id=1, source_target_pairs={{0,1},{1,2},{2,3},{3,4},{4,5},{5,6},{6,7},{7,0},{8,9},{9,10},{10,1... | collective-permute-start | bytes 1966088 | tf_op jit(solution)/shard_map/ppermute | solution.py:264
  47.5 39.6 %collective-permute-start.6 = (bf16[2176,128]{1,0:T(8,128)(2,1)S(1)}, bf16[2176,128]{1,0:T(8,128)(2,1)S(1)}, u32[]{:S(2)}, u32[]{:S(2)}) collective-permute-start(bf16[2176,128]{1,0:T(8,128)(2,1)S(1)} %slice_select_fusion), channel_id=1, source_target_pairs={{1,0},{2,1},{3,2},{4,3},{5,4},{6,5},{7,6},{0,7},{9,8},{10,9},{11,1... | collective-permute-start | bytes 1671176 | tf_op jit(solution)/shard_map/ppermute | solution.py:264
  54.5 32.5 %collective-permute-start.7 = (bf16[1280,128]{1,0:T(8,128)(2,1)S(1)}, bf16[1280,128]{1,0:T(8,128)(2,1)S(1)}, u32[]{:S(2)}, u32[]{:S(2)}) collective-permute-start(bf16[1280,128]{1,0:T(8,128)(2,1)S(1)} %get-tuple-element.24), channel_id=1, source_target_pairs={{0,1},{1,2},{2,3},{3,4},{4,5},{5,6},{6,7},{7,8},{8,9},{9,10},{10,1... | collective-permute-start | bytes 983048 | tf_op jit(solution)/shard_map/ppermute | solution.py:264
  56.5 14.2 %collective-permute-start.8 = (bf16[768,128]{1,0:T(8,128)(2,1)S(1)}, bf16[768,128]{1,0:T(8,128)(2,1)S(1)}, u32[]{:S(2)}, u32[]{:S(2)}) collective-permute-start(bf16[768,128]{1,0:T(8,128)(2,1)S(1)} %get-tuple-element.25), channel_id=1, source_target_pairs={{1,0},{2,1},{3,2},{4,3},{5,4},{6,5},{7,6},{8,7},{9,8},{10,9},{11,1... | collective-permute-start | bytes 589832 | tf_op jit(solution)/shard_map/ppermute | solution.py:264

commit v3 on v2

--- a/solution.py
+++ b/solution.py
@@ -27,8 +27,8 @@
 L_TOP = [p for p in LOWER if p[0] < 3]
 R_REST = of("yD", FULL) + of("zU", UPPER) + of("zD", FULL)
 L_REST = of("yD", [(r, c) for r in range(3) for c in range(3)]) + of("zL", L_TOP) + of("zD", FULL[:12])
-R2, R3 = R_REST[:18], R_REST[18:]
-L2, L3 = L_REST[:13], L_REST[13:]
+R2, R3 = R_REST[:16], R_REST[16:]
+L2, L3 = of("sum", UPPER) + L_REST[:13], L_REST[13:]
 COLUMN = {"L": 0, "D": S, "U": 2 * S}
 QUADS = {
     "L": ((0, 0), (0, 1), (1, 1)),
@@ -48,6 +48,8 @@
 
 def unpack(message, ref, into):
     for i, (name, r, c) in enumerate(message):
+        if into[name] is None:
+            continue
         target, column = into[name]
         target[rows(r), pl.ds(column + c * B, B)] = ref[rows(i), :]
 
@@ -58,9 +60,9 @@
             target[rows(r), pl.ds(column + c * B, B)] = jnp.zeros((B, B), target.dtype)
 
 
-def product(acc, part, *terms):
+def product(acc, part, *terms, base=None):
     for i, n in QUADS[part]:
-        total = None
+        total = None if base is None else base[pl.ds(i * H, H), pl.ds(n * H, H)]
         for (left, lc, lp), (right, rc, rp) in terms:
             ks = [k for k in (0, 1) if (i, k) in QUADS[lp] and (k, n) in QUADS[rp]]
             if not ks:
@@ -88,7 +90,7 @@
     return block if flag is True else jnp.where(flag, block, jnp.zeros_like(block))
 
 
-def pack_kernel(edge, pattern, y, z, r1, l1, r2, l2, r3, l3, zz, yw, zw, yin, zin, sems):
+def pack_kernel(edge, pattern, y, z, r1, l1, r2, r3, l3, zz, yw, zw, yin, zin, sems):
     copies = []
     for i, (source, target) in enumerate(((y, yin), (z, zin))):
         for r in range(4):
@@ -110,7 +112,7 @@
             wide = yw if name[0] == "y" else zw
             ref[rows(i), :] = wide[rows(r), pl.ds(COLUMN[name[1]] + c * B, B)]
 
-    for message, ref in ((R1, r1), (L1, l1), (R2, r2), (L2, l2), (R3, r3), (L3, l3)):
+    for message, ref in ((R1, r1), (L1, l1), (R2, r2), (R3, r3), (L3, l3)):
         fill(message, ref)
 
     @pl.when(edge[0] == 1)
@@ -154,54 +156,67 @@
         product(acc, part, (side(left, part, 0), side(td, "D", 0)))
         for i, (r, c) in enumerate(BLOCKS[part]):
             out[rows(i), :] = acc[rows(r), rows(c)].astype(BF)
-
-
-def last_kernel(pattern, yw, zw, td, r1, l1, r2, l2, r3, l3, e, l, yout, zout, *scratch):
-    ya, yc, za, zc, tw, tua, tlc, acc, yo, zo, sems = scratch
-    for big in (ya, za):
-        clear(big, S, UPPER)
-    clear(yc, 0, LOWER)
+    for i, (name, r, c) in enumerate(L2):
+        if name != "sum":
+            wide = yw if name[0] == "y" else zw
+            l[rows(i), :] = wide[rows(r), pl.ds(COLUMN[name[1]] + c * B, B)]
+
+
+def relay_kernel(edge, zz, after, r3, l3, r3_out, l3_out):
+    @pl.when(edge[1] == 1)
+    def _():
+        r3_out[...] = zz[...]
+
+    @pl.when(edge[0] == 1)
+    def _():
+        l3_out[...] = zz[pl.ds(0, len(L3) * B), :]
+
+
+def own_kernel(pattern, yw, zw, td, r2, tl, *rest):
+    *sums, ya, acc = rest
+    unpack(R2, r2, {"yD": (ya, 0), "zU": None})
+    clear(tl, 0, LOWER)
+    y_d, z_d, t_d = side(yw, "D"), side(zw, "D"), side(td, "D", 0)
+    product(acc, "L", (side(zw, "L"), side(ya, "D", 0)), (z_d, side(yw, "L")))
+    for r, c in LOWER:
+        tl[rows(r), rows(c)] = masked(keep(pattern, "L", r, c), -0.5 * acc[rows(r), rows(c)]).astype(BF)
+    zl, zd, zu, yl, yd, zy = sums
+    product(zl, "L", (t_d, side(zw, "L")))
+    product(zd, "D", (t_d, z_d))
+    product(zu, "U", (t_d, side(zw, "U")))
+    product(yl, "L", (y_d, side(tl, "L", 0)))
+    product(yd, "D", (y_d, t_d))
+    product(zy, "U", (z_d, side(yw, "U")))
+
+
+def late_kernel(pattern, yw, zw, zy, yl, e, l2, tu, yu, yl_out, yc, acc):
+    unpack(L2, l2, {"yD": (yc, 0), "zL": None, "sum": None})
+    clear(yc, 0, [(r, c) for r in range(3) for c in range(3)])
+    clear(tu, 0, UPPER)
+    product(acc, "U", (side(zw, "U"), side(yc, "D", 0)), base=zy)
+    for r, c in UPPER:
+        tu[rows(r), rows(c)] = masked(keep(pattern, "U", r, c), -0.5 * acc[rows(r), rows(c)]).astype(BF)
+    product(yu, "U", (side(yw, "D"), side(tu, "U", 0)))
+    for total, blocks, message in ((yl_out, LOWER, e), (yu, UPPER, l2)):
+        for i, (r, c) in enumerate(blocks):
+            total[rows(r), rows(c)] += message[rows(i), :].astype(F32)
+
+
+def last_kernel(pattern, yw, tl, tu, zl, zd, zu, yl, yd, yu, r1, l1, r2, l2, r3, l3, yout, zout, *scratch):
+    yu_a, yl_c, za, zc, tua, tlc, acc, yo, zo, sems = scratch
+    clear(yu_a, 0, UPPER)
+    clear(za, S, UPPER)
+    clear(yl_c, 0, LOWER)
     clear(zc, 0, L_TOP)
-    clear(yc, S, [(r, c) for r in range(3) for c in range(3)])
     clear(zc, S, FULL[:12])
-    left = {"yD": (ya, 0), "yU": (ya, S), "zD": (za, 0), "zU": (za, S)}
-    right = {"yL": (yc, 0), "yD": (yc, S), "zL": (zc, 0), "zD": (zc, S)}
+    left = {"yD": None, "yU": (yu_a, 0), "zD": (za, 0), "zU": (za, S)}
+    right = {"yL": (yl_c, 0), "yD": None, "zL": (zc, 0), "zD": (zc, S), "sum": None}
     for message, ref in ((R1, r1), (R2, r2), (R3, r3)):
         unpack(message, ref, left)
     for message, ref in ((L1, l1), (L2, l2), (L3, l3)):
         unpack(message, ref, right)
-    clear(tw, COLUMN["L"], LOWER)
-    clear(tw, COLUMN["U"], UPPER)
     clear(tua, 0, UPPER)
     clear(tlc, 0, L_TOP)
-    product(acc, "L", (side(zw, "L"), side(ya, "D", 0)), (side(zw, "D"), side(yw, "L")))
-    for r, c in LOWER:
-        tw[rows(r), rows(c)] = masked(keep(pattern, "L", r, c), -0.5 * acc[rows(r), rows(c)]).astype(BF)
-    product(acc, "U", (side(zw, "D"), side(yw, "U")), (side(zw, "U"), side(yc, "D", S)))
-    for r, c in UPPER:
-        tw[rows(r), pl.ds(2 * S + c * B, B)] = masked(
-            keep(pattern, "U", r, c), -0.5 * acc[rows(r), rows(c)]
-        ).astype(BF)
-    left_mask = r1[pl.ds(len(R1) * B, 16), :].astype(F32)
-    right_mask = l1[pl.ds(len(L1) * B, 16), :].astype(F32)
-    product(acc, "U", (side(za, "D", 0), side(ya, "U", S)), (side(za, "U", S), side(yw, "D")))
-    for i, (r, c) in enumerate(UPPER):
-        tua[rows(r), rows(c)] = (-0.5 * acc[rows(r), rows(c)] * left_mask[i : i + 1, :]).astype(BF)
-    product(acc, "L", (side(zc, "L", 0), side(yw, "D")), (side(zc, "D", S), side(yc, "L", 0)))
-    for i, (r, c) in enumerate(LOWER):
-        if r < 3:
-            tlc[rows(r), rows(c)] = (-0.5 * acc[rows(r), rows(c)] * right_mask[i : i + 1, :]).astype(BF)
-
-    t_l, t_u, t_d = side(tw, "L"), side(tw, "U"), side(td, "D", 0)
-
-    def finish(out, part, *terms, extra=None):
-        product(acc, part, *terms)
-        for i, (r, c) in enumerate(BLOCKS[part]):
-            block = acc[rows(r), rows(c)]
-            if extra is not None:
-                block = block + extra[rows(i), :].astype(F32)
-            out[r, slot(part, r, c)] = masked(keep(pattern, part, r, c), block).astype(BF)
-
     copies = []
 
     def write(source, target):
@@ -209,15 +224,30 @@
             copies.append(pltpu.make_async_copy(source.at[r], target.at[r], sems.at[len(copies)]))
             copies[-1].start()
 
-    finish(zo, "L", (t_l, side(za, "D", 0)), (t_d, side(zw, "L")))
-    finish(zo, "D", (t_l, side(za, "U", S)), (t_d, side(zw, "D")), (t_u, side(zc, "L", 0)))
-    finish(zo, "U", (t_d, side(zw, "U")), (t_u, side(zc, "D", S)))
+    def finish(out, part, *terms, base):
+        if terms:
+            product(acc, part, *terms, base=base)
+        for r, c in BLOCKS[part]:
+            block = (acc if terms else base)[rows(r), rows(c)]
+            out[r, slot(part, r, c)] = masked(keep(pattern, part, r, c), block).astype(BF)
+
+    t_l, t_u = side(tl, "L", 0), side(tu, "U", 0)
+    finish(zo, "L", (t_l, side(za, "D", 0)), base=zl)
+    finish(zo, "D", (t_l, side(za, "U", S)), (t_u, side(zc, "L", 0)), base=zd)
+    finish(zo, "U", (t_u, side(zc, "D", S)), base=zu)
     write(zo, zout)
-    finish(
-        yo, "D", (side(yw, "L"), side(tua, "U", 0)), (side(yw, "D"), t_d), (side(yw, "U"), side(tlc, "L", 0))
-    )
-    finish(yo, "L", (side(yw, "D"), t_l), extra=e)
-    finish(yo, "U", (side(yw, "D"), t_u), extra=l)
+    left_mask = r1[pl.ds(len(R1) * B, 16), :].astype(F32)
+    right_mask = l1[pl.ds(len(L1) * B, 16), :].astype(F32)
+    product(acc, "U", (side(za, "D", 0), side(yu_a, "U", 0)), (side(za, "U", S), side(yw, "D")))
+    for i, (r, c) in enumerate(UPPER):
+        tua[rows(r), rows(c)] = (-0.5 * acc[rows(r), rows(c)] * left_mask[i : i + 1, :]).astype(BF)
+    product(acc, "L", (side(zc, "L", 0), side(yw, "D")), (side(zc, "D", S), side(yl_c, "L", 0)))
+    for i, (r, c) in enumerate(LOWER):
+        if r < 3:
+            tlc[rows(r), rows(c)] = (-0.5 * acc[rows(r), rows(c)] * right_mask[i : i + 1, :]).astype(BF)
+    finish(yo, "D", (side(yw, "L"), side(tua, "U", 0)), (side(yw, "U"), side(tlc, "L", 0)), base=yd)
+    finish(yo, "L", base=yl)
+    finish(yo, "U", base=yu)
     write(yo, yout)
     for copy in copies:
         copy.wait()
@@ -226,13 +256,14 @@
 VMEM = pl.BlockSpec(memory_space=pltpu.VMEM)
 SMEM = pl.BlockSpec(memory_space=pltpu.SMEM)
 ANY = pl.BlockSpec(memory_space=pl.ANY)
+HBM = pl.BlockSpec(memory_space=pltpu.HBM)
 
 
 def packed(blocks, masks=False):
     return jax.ShapeDtypeStruct((len(blocks) * B + 16 * masks, B), BF)
 
 
-def call(kernel, outs, out_specs, ins, scratch, flops, operands):
+def call(kernel, outs, out_specs, ins, scratch, flops, operands, **options):
     outs = tuple(outs)
     moved = sum(v.size * v.dtype.itemsize for v in (*outs, *operands))
     return pl.pallas_call(
@@ -243,10 +274,11 @@
         scratch_shapes=scratch,
         compiler_params=pltpu.CompilerParams(vmem_limit_bytes=VMEM_LIMIT),
         cost_estimate=pl.CostEstimate(flops=flops, bytes_accessed=moved, transcendentals=0),
+        **options,
     )(*operands)
 
 
-VMEM_LIMIT = 32 * 2**20
+VMEM_LIMIT = 24 * 2**20
 
 
 def local(ymatrix, zmatrix, pattern):
@@ -265,11 +297,11 @@
 
     wide = jax.ShapeDtypeStruct((S, 3 * S), BF)
     edge = jnp.stack([first, last]).astype(jnp.int32)
-    r1, l1, r2, l2, r3, l3, zz, yw, zw = call(
+    r1, l1, r2, r3, l3, zz, yw, zw = call(
         pack_kernel,
-        (packed(R1, True), packed(L1, True)) + tuple(packed(m) for m in (R2, L2, R3, L3, R3)) + (wide, wide),
-        [VMEM] * 9,
-        [SMEM, SMEM, ANY, ANY],
+        (packed(R1, True), packed(L1, True)) + tuple(packed(m) for m in (R2, R3, L3, R3)) + (wide, wide),
+        [VMEM] * 8,
+        [SMEM, SMEM, HBM, HBM],
         [
             pltpu.VMEM(ymatrix.shape, BF),
             pltpu.VMEM(ymatrix.shape, BF),
@@ -280,41 +312,60 @@
     )
     r1, l1 = send(r1, right), send(l1, left)
     zz = send(zz, ends)
-    r2, l2 = send(r2, right), send(l2, left)
-    td, e, l = call(
+    r2 = send(r2, right)
+    td, e, l2 = call(
         middle_kernel,
-        (jax.ShapeDtypeStruct((S, S), BF), packed(LOWER), packed(UPPER)),
+        (jax.ShapeDtypeStruct((S, S), BF), packed(LOWER), packed(L2)),
         [VMEM] * 3,
         [SMEM] + [VMEM] * 4,
         [pltpu.VMEM((S, S), BF), pltpu.VMEM((S, S), BF), pltpu.VMEM((S, S), F32)],
         6 * S**3,
         (pattern, yw, zw, r1, l1),
     )
-    e, l = send(e, right), send(l, left)
-    r3 = send(jnp.where(last, zz, r3), right_y)
-    l3 = send(jnp.where(first, zz[: len(L3) * B], l3), left_y)
+    e, l2 = send(e, right), send(l2, left)
+    r3, l3 = call(
+        relay_kernel,
+        (packed(R3), packed(L3)),
+        [VMEM] * 2,
+        [SMEM, VMEM, ANY, VMEM, VMEM],
+        [],
+        0,
+        (edge, zz, td, r3, l3),
+        input_output_aliases={3: 0, 4: 1},
+    )
+    r3, l3 = send(r3, right_y), send(l3, left_y)
+    square, total = jax.ShapeDtypeStruct((S, S), BF), jax.ShapeDtypeStruct((S, S), F32)
+    one, half = pltpu.VMEM((S, S), BF), pltpu.VMEM((S, 2 * S), BF)
+    full = pltpu.VMEM((S, S), F32)
+    tl, zl, zd, zu, yl, yd, zy = call(
+        own_kernel,
+        (square,) + (total,) * 6,
+        [VMEM] * 7,
+        [SMEM] + [VMEM] * 4,
+        [one, full],
+        10 * S**3,
+        (pattern, yw, zw, td, r2),
+    )
+    tu, yu, yl = call(
+        late_kernel,
+        (square, total, total),
+        [VMEM] * 3,
+        [SMEM] + [VMEM] * 6,
+        [one, full],
+        50 * S**3,
+        (pattern, yw, zw, zy, yl, e, l2),
+        input_output_aliases={4: 2},
+    )
     whole = jax.ShapeDtypeStruct(ymatrix.shape, BF)
-    half = pltpu.VMEM((S, 2 * S), BF)
+    block_rows = pltpu.VMEM(ymatrix.shape, BF)
     return call(
         last_kernel,
         (whole, whole),
         [ANY] * 2,
-        [SMEM] + [VMEM] * 11,
-        [
-            half,
-            half,
-            half,
-            half,
-            pltpu.VMEM((S, 3 * S), BF),
-            pltpu.VMEM((S, S), BF),
-            pltpu.VMEM((S, S), BF),
-            pltpu.VMEM((S, S), F32),
-            pltpu.VMEM(ymatrix.shape, BF),
-            pltpu.VMEM(ymatrix.shape, BF),
-            pltpu.SemaphoreType.DMA((8,)),
-        ],
-        20 * S**3,
-        (pattern, yw, zw, td, r1, l1, r2, l2, r3, l3, e, l),
+        [SMEM] + [VMEM] * 15,
+        [one, one, half, half, one, one, full, block_rows, block_rows, pltpu.SemaphoreType.DMA((8,))],
+        10 * S**3,
+        (pattern, yw, tl, tu, zl, zd, zu, yl, yd, yu, r1, l1, r2, l2, r3, l3),
     )
 
 

time: 93.6 us -> 86 us (0.919); the launches traced: 93.1 us -> 84.3 us
  starting transfers between devices: 46.3 us -> 33.1 us
  waiting for transfers between devices: 32.8 us -> 35.2 us
  Pallas kernels: 9.92 us -> 12.1 us
    ppermute x9 -> x8, starting transfers between devices: 46.3 us -> 33.1 us  [send(): return lax.ppermute(x, AXES, pairs)]
    ppermute x9 -> x8, waiting for transfers between devices: 32.8 us -> 35.2 us  [send(): return lax.ppermute(x, AXES, pairs)]
    pallas_call x3 -> x6, Pallas kernels: 9.92 us -> 12.1 us  [call(): pl.pallas_call(kernel, out_shape=outs, in_specs=ins, out_specs=tuple(out_...]
  transfers between devices with their start and end apart: 9 -> 8, of which waited for: 3 -> 6; matrix products, arithmetic and copies ran while one was open for 0% -> 0% of each run, Pallas kernels for 2% -> 7%
where the time goes in v3:
time: 86 us; the launch traced here: 84.3 us
  waiting for transfers between devices  35.2 us (41%)
  starting transfers between devices  33.1 us (38%)
  Pallas kernels  12.1 us (14%)
  local copies, waits for them, and re-layouts  3.14 us (4%)
    ppermute x8, waiting for transfers between devices, send(): return lax.ppermute(x, AXES, pairs)  35.2 us
    ppermute x8, starting transfers between devices, send(): return lax.ppermute(x, AXES, pairs)  33.1 us
    pallas_call x6, Pallas kernels, call(): pl.pallas_call(kernel, out_shape=outs, in_specs=ins, out_specs=tuple(out_...  12.1 us
    unnamed x8, local copies, waits for them, and re-layouts  3.14 us
  transfers between devices with their start and end apart: 8, of which 6 were waited for; matrix products, arithmetic and copies ran while one was open for 0% of the time, Pallas kernels for 7%

profile of v3, /device:TPU:6, one launch (start us, length us, event | category | flops | bytes accessed | tf_op | source)
XLA Modules:
  0.0 84.3 jit_solution(17950147694486559478)
XLA Ops:
  0.6 0.0 copy-start.3
  0.7 0.1 add_convert_fusion.edge
  0.7 0.0 copy-start
  0.7 1.2 %copy-done = bf16[4,8,128,128]{3,2,1,0:T(8,128)(2,1)S(1)} copy-done((bf16[4,8,128,128]{3,2,1,0:T(8,128)(2,1)S(1)}, bf16[4,8,128,128]{3,2,1,0:T(8,128)(2,1)}, u32[]{:S(2)}) %copy-start) | copy-done | bytes 1048600
  2.0 0.0 copy-start.1
  2.0 1.2 %copy-done.1 = bf16[4,8,128,128]{3,2,1,0:T(8,128)(2,1)S(1)} copy-done((bf16[4,8,128,128]{3,2,1,0:T(8,128)(2,1)S(1)}, bf16[4,8,128,128]{3,2,1,0:T(8,128)(2,1)}, u32[]{:S(2)}) %copy-start.1) | copy-done | bytes 1048600
  3.2 0.0 copy-start.2
  3.2 0.7 copy-done.2
  3.9 1.9 %shard_map.50 = (bf16[784,128]{1,0:T(8,128)(2,1)S(1)}, bf16[1296,128]{1,0:T(8,128)(2,1)S(1)}, bf16[2048,128]{1,0:T(8,128)(2,1)S(1)}, bf16[2816,128]{1,0:T(8,128)...) custom-call(s32[2]{0:T(128)S(1)} %add_convert_fusion.edge, ...), custom_call_target="tpu_custom_call" | custom-call | bytes 8298632 | tf_op jit(solution)/shard_map/pallas_call | solution.py:269
  5.8 13.6 %collective-permute-start.1 = (bf16[1296,128]{1,0:T(8,128)(2,1)S(1)}, bf16[1296,128]{1,0:T(8,128)(2,1)S(1)}, u32[]{:S(2)}, u32[]{:S(2)}) collective-permute-start(bf16[1296,128]{1,0:T(8,128)(2,1)S(1)} %get-tuple-element.28), channel_id=1, source_target_pairs={{1,0},{2,1},{3,2},{4,3},{5,4},{6,5},{7,6},{8,7},{9,8},{10,9},{11,1... | collective-permute-start | bytes 995336 | tf_op jit(solution)/shard_map/ppermute | solution.py:296
  19.4 1.9 %collective-permute-start = (bf16[784,128]{1,0:T(8,128)(2,1)S(1)}, bf16[784,128]{1,0:T(8,128)(2,1)S(1)}, u32[]{:S(2)}, u32[]{:S(2)}) collective-permute-start(bf16[784,128]{1,0:T(8,128)(2,1)S(1)} %get-tuple-element.27), channel_id=1, source_target_pairs={{0,1},{1,2},{2,3},{3,4},{4,5},{5,6},{6,7},{7,8},{8,9},{9,10},{10,1... | collective-permute-start | bytes 602120 | tf_op jit(solution)/shard_map/ppermute | solution.py:296
  21.3 2.2 %collective-permute-start.5 = (bf16[2816,128]{1,0:T(8,128)(2,1)S(1)}, bf16[2816,128]{1,0:T(8,128)(2,1)S(1)}, u32[]{:S(2)}, u32[]{:S(2)}) collective-permute-start(bf16[2816,128]{1,0:T(8,128)(2,1)S(1)} %get-tuple-element.43), channel_id=1, source_target_pairs={{7,15},{15,23},{23,31},{31,39},{39,47},{47,55},{55,63},{63,71},{71... | collective-permute-start | bytes 2162696 | tf_op jit(solution)/shard_map/ppermute | solution.py:296
  23.5 1.9 %collective-permute-start.2 = (bf16[2048,128]{1,0:T(8,128)(2,1)S(1)}, bf16[2048,128]{1,0:T(8,128)(2,1)S(1)}, u32[]{:S(2)}, u32[]{:S(2)}) collective-permute-start(bf16[2048,128]{1,0:T(8,128)(2,1)S(1)} %get-tuple-element.30), channel_id=1, source_target_pairs={{0,1},{1,2},{2,3},{3,4},{4,5},{5,6},{6,7},{7,8},{8,9},{9,10},{10,1... | collective-permute-start | bytes 1572872 | tf_op jit(solution)/shard_map/ppermute | solution.py:296
  25.4 13.3 %collective-permute-done.r1 = bf16[784,128]{1,0:T(8,128)(2,1)S(1)} collective-permute-done((bf16[784,128]{1,0:T(8,128)(2,1)S(1)}, bf16[784,128]{1,0:T(8,128)(2,1)S(1)}, u32[]{:S(2)}, u32[]{:S(2)}) %collective-permute-start) | collective-permute-done | bytes 200736 | tf_op jit(solution)/shard_map/ppermute | solution.py:296
  38.7 0.0 collective-permute-done.1.l1
  38.7 0.0 copy-done.3
  38.7 1.9 %shard_map.51 = (bf16[512,512]{1,0:T(8,128)(2,1)S(1)}, bf16[1280,128]{1,0:T(8,128)(2,1)S(1)}, bf16[2432,128]{1,0:T(8,128)(2,1)S(1)}) custom-call(s32[4,8]{1,0:T(4,128)S(1)} %copy-done.3, bf16[512,1536]{1,0:T(8,128)(2,1)S(1)} %get-tuple-element.25.yw, bf16[512,1536]{1,0:T(8,128)(2,1)S(1)} %get-tuple-element.26.zw, ...), custom_call_target="tpu_custom_call" | custom-call | flops 805306368 | bytes 5152896 | tf_op jit(solution)/shard_map/pallas_call | solution.py:269
  40.6 2.9 %collective-permute-start.4 = (bf16[2432,128]{1,0:T(8,128)(2,1)S(1)}, bf16[2432,128]{1,0:T(8,128)(2,1)S(1)}, u32[]{:S(2)}, u32[]{:S(2)}) collective-permute-start(bf16[2432,128]{1,0:T(8,128)(2,1)S(1)} %get-tuple-element.35), channel_id=1, source_target_pairs={{1,0},{2,1},{3,2},{4,3},{5,4},{6,5},{7,6},{8,7},{9,8},{10,9},{11,1... | collective-permute-start | bytes 1867784 | tf_op jit(solution)/shard_map/ppermute | solution.py:296
  43.5 2.9 %collective-permute-start.3 = (bf16[1280,128]{1,0:T(8,128)(2,1)S(1)}, bf16[1280,128]{1,0:T(8,128)(2,1)S(1)}, u32[]{:S(2)}, u32[]{:S(2)}) collective-permute-start(bf16[1280,128]{1,0:T(8,128)(2,1)S(1)} %get-tuple-element.34), channel_id=1, source_target_pairs={{0,1},{1,2},{2,3},{3,4},{4,5},{5,6},{6,7},{7,8},{8,9},{9,10},{10,1... | collective-permute-start | bytes 983048 | tf_op jit(solution)/shard_map/ppermute | solution.py:296
  46.4 11.7 %collective-permute-done.5.zz = bf16[2816,128]{1,0:T(8,128)(2,1)S(1)} collective-permute-done((bf16[2816,128]{1,0:T(8,128)(2,1)S(1)}, bf16[2816,128]{1,0:T(8,128)(2,1)S(1)}, u32[]{:S(2)}, u32[]{:S(2)}) %collective-permute-start.5) | collective-permute-done | bytes 720928 | tf_op jit(solution)/shard_map/ppermute | solution.py:296
  58.2 0.6 shard_map.54
  58.8 1.9 %collective-permute-start.6 = (bf16[2816,128]{1,0:T(8,128)(2,1)S(1)}, bf16[2816,128]{1,0:T(8,128)(2,1)S(1)}, u32[]{:S(2)}, u32[]{:S(2)}) collective-permute-start(bf16[2816,128]{1,0:T(8,128)(2,1)S(1)} %get-tuple-element.46), channel_id=1, source_target_pairs={{0,1},{1,2},{2,3},{3,4},{4,5},{5,6},{6,7},{7,0},{8,9},{9,10},{10,1... | collective-permute-start | bytes 2162696 | tf_op jit(solution)/shard_map/ppermute | solution.py:296
  60.7 0.8 collective-permute-done.2.r2
  61.4 2.3 %shard_map.52 = (bf16[512,512]{1,0:T(8,128)(2,1)S(1)}, f32[512,512]{1,0:T(8,128)S(1)}, f32[512,512]{1,0:T(8,128)S(1)}, f32[512,512]{1,0:T(8,128)S(1)}, f32[512,5...) custom-call(s32[4,8]{1,0:T(4,128)S(1)} %copy-done.3, bf16[512,1536]{1,0:T(8,128)(2,1)S(1)} %get-tuple-element.25.yw, ...), custom_call_target="tpu_custom_call" | custom-call | flops 1342177280 | bytes 11010176 | tf_op jit(solution)/shard_map/pallas_call | solution.py:269
  63.8 5.7 %collective-permute-start.7 = (bf16[2176,128]{1,0:T(8,128)(2,1)S(1)}, bf16[2176,128]{1,0:T(8,128)(2,1)S(1)}, u32[]{:S(2)}, u32[]{:S(2)}) collective-permute-start(bf16[2176,128]{1,0:T(8,128)(2,1)S(1)} %get-tuple-element.47), channel_id=1, source_target_pairs={{1,0},{2,1},{3,2},{4,3},{5,4},{6,5},{7,6},{0,7},{9,8},{10,9},{11,1... | collective-permute-start | bytes 1671176 | tf_op jit(solution)/shard_map/ppermute | solution.py:296
  69.5 4.9 %collective-permute-done.3.e = bf16[1280,128]{1,0:T(8,128)(2,1)S(1)} collective-permute-done((bf16[1280,128]{1,0:T(8,128)(2,1)S(1)}, bf16[1280,128]{1,0:T(8,128)(2,1)S(1)}, u32[]{:S(2)}, u32[]{:S(2)}) %collective-permute-start.3) | collective-permute-done | bytes 327712 | tf_op jit(solution)/shard_map/ppermute | solution.py:296
  74.4 0.0 collective-permute-done.4.l2
  74.4 1.3 %shard_map.53 = (bf16[512,512]{1,0:T(8,128)(2,1)S(1)}, f32[512,512]{1,0:T(8,128)S(1)}, f32[512,512]{1,0:T(8,128)S(1)}) custom-call(s32[4,8]{1,0:T(4,128)S(1)} %copy-done.3, bf16[512,1536]{1,0:T(8,128)(2,1)S(1)} %get-tuple-element.25.yw, bf16[512,1536]{1,0:T(8,128)(2,1)S(1)} %get-tuple-element.26.zw, ...), custom_call_target="tpu_custom_call", output_to_operand_aliasing={{2}: (4, {})} | custom-call | flops 6710886400 | bytes 8814720 | tf_op jit(solution)/shard_map/pallas_call | solution.py:269
  75.7 3.8 %collective-permute-done.7.l3 = bf16[2176,128]{1,0:T(8,128)(2,1)S(1)} collective-permute-done((bf16[2176,128]{1,0:T(8,128)(2,1)S(1)}, bf16[2176,128]{1,0:T(8,128)(2,1)S(1)}, u32[]{:S(2)}, u32[]{:S(2)}) %collective-permute-start.7) | collective-permute-done | bytes 557088 | tf_op jit(solution)/shard_map/ppermute | solution.py:296
  79.6 0.7 collective-permute-done.6.r3
  80.2 4.1 %shard_map.55 = (bf16[4,8,128,128]{3,2,1,0:T(8,128)(2,1)}, bf16[4,8,128,128]{3,2,1,0:T(8,128)(2,1)}) custom-call(s32[4,8]{1,0:T(4,128)S(1)} %copy-done.3, bf16[512,1536]{1,0:T(8,128)(2,1)S(1)} %get-tuple-element.25.yw, bf16[512,512]{1,0:T(8,128)(2,1)S(1)} %get-tuple-element.31.tl, bf16[512,512]{1,0:T(8,128)(2,1)S(1)} %get-tuple-element.36.tu, ...), custom_call_target="tpu_custom_call" | custom-call | flops 1342177280 | bytes 13967488 | tf_op jit(solution)/shard_map/pallas_call | solution.py:269
Async XLA Ops:
  0.6 38.0 %copy-start.3 = (s32[4,8]{1,0:T(4,128)S(1)}, s32[4,8]{1,0:T(4,128)}, u32[]{:S(2)}) copy-start(s32[4,8]{1,0:T(4,128)} %pattern.9) | copy-start | bytes 388
  0.7 1.2 %copy-start = (bf16[4,8,128,128]{3,2,1,0:T(8,128)(2,1)S(1)}, bf16[4,8,128,128]{3,2,1,0:T(8,128)(2,1)}, u32[]{:S(2)}) copy-start(bf16[4,8,128,128]{3,2,1,0:T(8,128)(2,1)} %y.1) | copy-start | bytes 3145732
  2.0 1.2 %copy-start.1 = (bf16[4,8,128,128]{3,2,1,0:T(8,128)(2,1)S(1)}, bf16[4,8,128,128]{3,2,1,0:T(8,128)(2,1)}, u32[]{:S(2)}) copy-start(bf16[4,8,128,128]{3,2,1,0:T(8,128)(2,1)} %z.1) | copy-start | bytes 3145732
  3.2 0.7 copy-start.2
  5.8 32.9 %collective-permute-start.1 = (bf16[1296,128]{1,0:T(8,128)(2,1)S(1)}, bf16[1296,128]{1,0:T(8,128)(2,1)S(1)}, u32[]{:S(2)}, u32[]{:S(2)}) collective-permute-start(bf16[1296,128]{1,0:T(8,128)(2,1)S(1)} %get-tuple-element.28), channel_id=1, source_target_pairs={{1,0},{2,1},{3,2},{4,3},{5,4},{6,5},{7,6},{8,7},{9,8},{10,9},{11,1... | collective-permute-start | bytes 995336 | tf_op jit(solution)/shard_map/ppermute | solution.py:296
  19.4 19.3 %collective-permute-start = (bf16[784,128]{1,0:T(8,128)(2,1)S(1)}, bf16[784,128]{1,0:T(8,128)(2,1)S(1)}, u32[]{:S(2)}, u32[]{:S(2)}) collective-permute-start(bf16[784,128]{1,0:T(8,128)(2,1)S(1)} %get-tuple-element.27), channel_id=1, source_target_pairs={{0,1},{1,2},{2,3},{3,4},{4,5},{5,6},{6,7},{7,8},{8,9},{9,10},{10,1... | collective-permute-start | bytes 602120 | tf_op jit(solution)/shard_map/ppermute | solution.py:296
  21.3 36.9 %collective-permute-start.5 = (bf16[2816,128]{1,0:T(8,128)(2,1)S(1)}, bf16[2816,128]{1,0:T(8,128)(2,1)S(1)}, u32[]{:S(2)}, u32[]{:S(2)}) collective-permute-start(bf16[2816,128]{1,0:T(8,128)(2,1)S(1)} %get-tuple-element.43), channel_id=1, source_target_pairs={{7,15},{15,23},{23,31},{31,39},{39,47},{47,55},{55,63},{63,71},{71... | collective-permute-start | bytes 2162696 | tf_op jit(solution)/shard_map/ppermute | solution.py:296
  23.5 38.0 %collective-permute-start.2 = (bf16[2048,128]{1,0:T(8,128)(2,1)S(1)}, bf16[2048,128]{1,0:T(8,128)(2,1)S(1)}, u32[]{:S(2)}, u32[]{:S(2)}) collective-permute-start(bf16[2048,128]{1,0:T(8,128)(2,1)S(1)} %get-tuple-element.30), channel_id=1, source_target_pairs={{0,1},{1,2},{2,3},{3,4},{4,5},{5,6},{6,7},{7,8},{8,9},{9,10},{10,1... | collective-permute-start | bytes 1572872 | tf_op jit(solution)/shard_map/ppermute | solution.py:296
  40.6 33.9 %collective-permute-start.4 = (bf16[2432,128]{1,0:T(8,128)(2,1)S(1)}, bf16[2432,128]{1,0:T(8,128)(2,1)S(1)}, u32[]{:S(2)}, u32[]{:S(2)}) collective-permute-start(bf16[2432,128]{1,0:T(8,128)(2,1)S(1)} %get-tuple-element.35), channel_id=1, source_target_pairs={{1,0},{2,1},{3,2},{4,3},{5,4},{6,5},{7,6},{8,7},{9,8},{10,9},{11,1... | collective-permute-start | bytes 1867784 | tf_op jit(solution)/shard_map/ppermute | solution.py:296
  43.5 30.9 %collective-permute-start.3 = (bf16[1280,128]{1,0:T(8,128)(2,1)S(1)}, bf16[1280,128]{1,0:T(8,128)(2,1)S(1)}, u32[]{:S(2)}, u32[]{:S(2)}) collective-permute-start(bf16[1280,128]{1,0:T(8,128)(2,1)S(1)} %get-tuple-element.34), channel_id=1, source_target_pairs={{0,1},{1,2},{2,3},{3,4},{4,5},{5,6},{6,7},{7,8},{8,9},{9,10},{10,1... | collective-permute-start | bytes 983048 | tf_op jit(solution)/shard_map/ppermute | solution.py:296
  58.8 21.5 %collective-permute-start.6 = (bf16[2816,128]{1,0:T(8,128)(2,1)S(1)}, bf16[2816,128]{1,0:T(8,128)(2,1)S(1)}, u32[]{:S(2)}, u32[]{:S(2)}) collective-permute-start(bf16[2816,128]{1,0:T(8,128)(2,1)S(1)} %get-tuple-element.46), channel_id=1, source_target_pairs={{0,1},{1,2},{2,3},{3,4},{4,5},{5,6},{6,7},{7,0},{8,9},{9,10},{10,1... | collective-permute-start | bytes 2162696 | tf_op jit(solution)/shard_map/ppermute | solution.py:296
  63.8 15.8 %collective-permute-start.7 = (bf16[2176,128]{1,0:T(8,128)(2,1)S(1)}, bf16[2176,128]{1,0:T(8,128)(2,1)S(1)}, u32[]{:S(2)}, u32[]{:S(2)}) collective-permute-start(bf16[2176,128]{1,0:T(8,128)(2,1)S(1)} %get-tuple-element.47), channel_id=1, source_target_pairs={{1,0},{2,1},{3,2},{4,3},{5,4},{6,5},{7,6},{0,7},{9,8},{10,9},{11,1... | collective-permute-start | bytes 1671176 | tf_op jit(solution)/shard_map/ppermute | solution.py:296

commit v4 on v3

--- a/solution.py
+++ b/solution.py
@@ -27,8 +27,8 @@
 L_TOP = [p for p in LOWER if p[0] < 3]
 R_REST = of("yD", FULL) + of("zU", UPPER) + of("zD", FULL)
 L_REST = of("yD", [(r, c) for r in range(3) for c in range(3)]) + of("zL", L_TOP) + of("zD", FULL[:12])
-R2, R3 = R_REST[:16], R_REST[16:]
-L2, L3 = of("sum", UPPER) + L_REST[:13], L_REST[13:]
+R2, R3 = R_REST[:18], R_REST[18:]
+L2, L3 = of("sum", UPPER) + L_REST[:15], L_REST[15:]
 COLUMN = {"L": 0, "D": S, "U": 2 * S}
 QUADS = {
     "L": ((0, 0), (0, 1), (1, 1)),
@@ -90,22 +90,24 @@
     return block if flag is True else jnp.where(flag, block, jnp.zeros_like(block))
 
 
-def pack_kernel(edge, pattern, y, z, r1, l1, r2, r3, l3, zz, yw, zw, yin, zin, sems):
-    copies = []
+def pack_kernel(pattern_in, y, z, r1, l1, r2, r3, l3, zz, yw, zw, yin, zin, pattern, sems):
+    place = lax.rem(lax.axis_index("col"), RING)
+    copies = [pltpu.make_async_copy(pattern_in, pattern, sems.at[8])]
     for i, (source, target) in enumerate(((y, yin), (z, zin))):
         for r in range(4):
             copies.append(pltpu.make_async_copy(source.at[r], target.at[r], sems.at[i * 4 + r]))
-            copies[-1].start()
     for copy in copies:
-        copy.wait()
-    for wide, source in ((yw, yin), (zw, zin)):
+        copy.start()
+    copies[0].wait()
+    for i, (wide, source) in enumerate(((yw, yin), (zw, zin))):
         for r in range(4):
+            for c in range(12):
+                if not r <= c < r + 8:
+                    wide[rows(r), rows(c)] = jnp.zeros((B, B), BF)
+            copies[1 + i * 4 + r].wait()
             for d in range(8):
                 k = True if d == 4 else pattern[r, d] == 1
                 wide[rows(r), rows(r + d)] = masked(k, source[r, d])
-            for c in range(12):
-                if not r <= c < r + 8:
-                    wide[rows(r), rows(c)] = jnp.zeros((B, B), BF)
 
     def fill(message, ref):
         for i, (name, r, c) in enumerate(message):
@@ -115,11 +117,11 @@
     for message, ref in ((R1, r1), (L1, l1), (R2, r2), (R3, r3), (L3, l3)):
         fill(message, ref)
 
-    @pl.when(edge[0] == 1)
+    @pl.when(place == 0)
     def _():
         fill(L3, zz)
 
-    @pl.when(edge[0] == 0)
+    @pl.when(place == RING - 1)
     def _():
         fill(R3, zz)
 
@@ -162,14 +164,24 @@
             l[rows(i), :] = wide[rows(r), pl.ds(COLUMN[name[1]] + c * B, B)]
 
 
-def relay_kernel(edge, zz, after, r3, l3, r3_out, l3_out):
-    @pl.when(edge[1] == 1)
-    def _():
-        r3_out[...] = zz[...]
-
-    @pl.when(edge[0] == 1)
+def relay_kernel(zz, after, r3, l3, r3_out, l3_out):
+    place = lax.rem(lax.axis_index("col"), RING)
+
+    @pl.when(place == RING - 1)
+    def _():
+        r3_out[...] = zz[pl.ds(0, len(R3) * B), :]
+
+    @pl.when(place != RING - 1)
+    def _():
+        r3_out[...] = r3[...]
+
+    @pl.when(place == 0)
     def _():
         l3_out[...] = zz[pl.ds(0, len(L3) * B), :]
+
+    @pl.when(place != 0)
+    def _():
+        l3_out[...] = l3[...]
 
 
 def own_kernel(pattern, yw, zw, td, r2, tl, *rest):
@@ -189,66 +201,84 @@
     product(zy, "U", (z_d, side(yw, "U")))
 
 
-def late_kernel(pattern, yw, zw, zy, yl, e, l2, tu, yu, yl_out, yc, acc):
+def finish(pattern, out, total, part, extra=None):
+    for i, (r, c) in enumerate(BLOCKS[part]):
+        block = total[rows(r), rows(c)]
+        if extra is not None:
+            block = block + extra[rows(i), :].astype(F32)
+        out[i] = masked(keep(pattern, part, r, c), block).astype(BF)
+
+
+def late_kernel(pattern, yw, zw, zy, yl, e, l2, tu, yl_out, yu_out, yc, acc):
     unpack(L2, l2, {"yD": (yc, 0), "zL": None, "sum": None})
     clear(yc, 0, [(r, c) for r in range(3) for c in range(3)])
     clear(tu, 0, UPPER)
+    finish(pattern, yl_out, yl, "L", e)
     product(acc, "U", (side(zw, "U"), side(yc, "D", 0)), base=zy)
     for r, c in UPPER:
         tu[rows(r), rows(c)] = masked(keep(pattern, "U", r, c), -0.5 * acc[rows(r), rows(c)]).astype(BF)
-    product(yu, "U", (side(yw, "D"), side(tu, "U", 0)))
-    for total, blocks, message in ((yl_out, LOWER, e), (yu, UPPER, l2)):
-        for i, (r, c) in enumerate(blocks):
-            total[rows(r), rows(c)] += message[rows(i), :].astype(F32)
-
-
-def last_kernel(pattern, yw, tl, tu, zl, zd, zu, yl, yd, yu, r1, l1, r2, l2, r3, l3, yout, zout, *scratch):
-    yu_a, yl_c, za, zc, tua, tlc, acc, yo, zo, sems = scratch
-    clear(yu_a, 0, UPPER)
-    clear(za, S, UPPER)
-    clear(yl_c, 0, LOWER)
-    clear(zc, 0, L_TOP)
-    clear(zc, S, FULL[:12])
-    left = {"yD": None, "yU": (yu_a, 0), "zD": (za, 0), "zU": (za, S)}
-    right = {"yL": (yl_c, 0), "yD": None, "zL": (zc, 0), "zD": (zc, S), "sum": None}
-    for message, ref in ((R1, r1), (R2, r2), (R3, r3)):
-        unpack(message, ref, left)
+    product(acc, "U", (side(yw, "D"), side(tu, "U", 0)))
+    finish(pattern, yu_out, acc, "U", l2)
+
+
+def right_kernel(pattern, yw, tu, zd, zu, yd, l1, l2, l3, zu_out, zd_out, yd_out, yl, zl_c, zd_c, tlc, acc):
+    clear(yl, 0, LOWER)
+    clear(zl_c, 0, L_TOP)
+    clear(zd_c, 0, FULL[:12])
     for message, ref in ((L1, l1), (L2, l2), (L3, l3)):
-        unpack(message, ref, right)
-    clear(tua, 0, UPPER)
+        unpack(message, ref, {"yL": (yl, 0), "yD": None, "zL": (zl_c, 0), "zD": (zd_c, 0), "sum": None})
     clear(tlc, 0, L_TOP)
-    copies = []
-
-    def write(source, target):
-        for r in range(4):
-            copies.append(pltpu.make_async_copy(source.at[r], target.at[r], sems.at[len(copies)]))
-            copies[-1].start()
-
-    def finish(out, part, *terms, base):
-        if terms:
-            product(acc, part, *terms, base=base)
-        for r, c in BLOCKS[part]:
-            block = (acc if terms else base)[rows(r), rows(c)]
-            out[r, slot(part, r, c)] = masked(keep(pattern, part, r, c), block).astype(BF)
-
-    t_l, t_u = side(tl, "L", 0), side(tu, "U", 0)
-    finish(zo, "L", (t_l, side(za, "D", 0)), base=zl)
-    finish(zo, "D", (t_l, side(za, "U", S)), (t_u, side(zc, "L", 0)), base=zd)
-    finish(zo, "U", (t_u, side(zc, "D", S)), base=zu)
-    write(zo, zout)
-    left_mask = r1[pl.ds(len(R1) * B, 16), :].astype(F32)
-    right_mask = l1[pl.ds(len(L1) * B, 16), :].astype(F32)
-    product(acc, "U", (side(za, "D", 0), side(yu_a, "U", 0)), (side(za, "U", S), side(yw, "D")))
-    for i, (r, c) in enumerate(UPPER):
-        tua[rows(r), rows(c)] = (-0.5 * acc[rows(r), rows(c)] * left_mask[i : i + 1, :]).astype(BF)
-    product(acc, "L", (side(zc, "L", 0), side(yw, "D")), (side(zc, "D", S), side(yl_c, "L", 0)))
+    mask = l1[pl.ds(len(L1) * B, 16), :].astype(F32)
+    product(acc, "L", (side(zl_c, "L", 0), side(yw, "D")), (side(zd_c, "D", 0), side(yl, "L", 0)))
     for i, (r, c) in enumerate(LOWER):
         if r < 3:
-            tlc[rows(r), rows(c)] = (-0.5 * acc[rows(r), rows(c)] * right_mask[i : i + 1, :]).astype(BF)
-    finish(yo, "D", (side(yw, "L"), side(tua, "U", 0)), (side(yw, "U"), side(tlc, "L", 0)), base=yd)
-    finish(yo, "L", base=yl)
-    finish(yo, "U", base=yu)
-    write(yo, yout)
+            tlc[rows(r), rows(c)] = (-0.5 * acc[rows(r), rows(c)] * mask[i : i + 1, :]).astype(BF)
+    t_u = side(tu, "U", 0)
+    product(acc, "U", (t_u, side(zd_c, "D", 0)), base=zu)
+    finish(pattern, zu_out, acc, "U")
+    product(zd_out, "D", (t_u, side(zl_c, "L", 0)), base=zd)
+    product(yd_out, "D", (side(yw, "U"), side(tlc, "L", 0)), base=yd)
+
+
+def last_kernel(pattern, yw, tl, zl, zd, zu, yl, yd, yu, r1, r2, r3, yout, zout, *scratch):
+    yu_a, zu_a, zd_a, tua, acc, y_d, z_d, z_l, sems = scratch
+    copies = []
+
+    def write(source, target, part):
+        at = 0
+        for r in range(4):
+            size, d = {"L": (4 - r, 0), "D": (4, 4 - r), "U": (r, 8 - r)}[part]
+            if size:
+                copies.append(
+                    pltpu.make_async_copy(
+                        source.at[pl.ds(at, size)], target.at[r, pl.ds(d, size)], sems.at[len(copies)]
+                    )
+                )
+                copies[-1].start()
+            at += size
+
+    write(zu, zout, "U")
+    write(yl, yout, "L")
+    write(yu, yout, "U")
+    clear(yu_a, 0, UPPER)
+    clear(zu_a, 0, UPPER)
+    for message, ref in ((R1, r1), (R2, r2), (R3, r3)):
+        unpack(message, ref, {"yD": None, "yU": (yu_a, 0), "zD": (zd_a, 0), "zU": (zu_a, 0)})
+    clear(tua, 0, UPPER)
+    mask = r1[pl.ds(len(R1) * B, 16), :].astype(F32)
+    t_l = side(tl, "L", 0)
+    product(acc, "D", (t_l, side(zu_a, "U", 0)), base=zd)
+    finish(pattern, z_d, acc, "D")
+    write(z_d, zout, "D")
+    product(acc, "U", (side(zd_a, "D", 0), side(yu_a, "U", 0)), (side(zu_a, "U", 0), side(yw, "D")))
+    for i, (r, c) in enumerate(UPPER):
+        tua[rows(r), rows(c)] = (-0.5 * acc[rows(r), rows(c)] * mask[i : i + 1, :]).astype(BF)
+    product(acc, "D", (side(yw, "L"), side(tua, "U", 0)), base=yd)
+    finish(pattern, y_d, acc, "D")
+    write(y_d, yout, "D")
+    product(acc, "L", (t_l, side(zd_a, "D", 0)), base=zl)
+    finish(pattern, z_l, acc, "L")
+    write(z_l, zout, "L")
     for copy in copies:
         copy.wait()
 
@@ -279,12 +309,11 @@
 
 
 VMEM_LIMIT = 24 * 2**20
+OWN_COST, LATE_COST, RIGHT_COST = 10, 35, 5
 
 
 def local(ymatrix, zmatrix, pattern):
     count = lax.axis_size("row") * lax.axis_size("col")
-    place = lax.axis_index("col") % RING
-    first, last = place == 0, place == RING - 1
     right = [(i, (i + 1) % count) for i in range(count)]
     left = [(b, a) for a, b in right]
     ends = [(i, (i + RING) % count) for i in range(count) if i % RING == RING - 1]
@@ -296,19 +325,19 @@
         return lax.ppermute(x, AXES, pairs)
 
     wide = jax.ShapeDtypeStruct((S, 3 * S), BF)
-    edge = jnp.stack([first, last]).astype(jnp.int32)
     r1, l1, r2, r3, l3, zz, yw, zw = call(
         pack_kernel,
-        (packed(R1, True), packed(L1, True)) + tuple(packed(m) for m in (R2, R3, L3, R3)) + (wide, wide),
+        (packed(R1, True), packed(L1, True)) + tuple(packed(m) for m in (R2, R3, L3, max(R3, L3, key=len))) + (wide, wide),
         [VMEM] * 8,
-        [SMEM, SMEM, HBM, HBM],
+        [HBM] * 3,
         [
             pltpu.VMEM(ymatrix.shape, BF),
             pltpu.VMEM(ymatrix.shape, BF),
-            pltpu.SemaphoreType.DMA((8,)),
+            pltpu.SMEM(pattern.shape, jnp.int32),
+            pltpu.SemaphoreType.DMA((9,)),
         ],
         0,
-        (edge, pattern, ymatrix, zmatrix),
+        tuple(pltpu.with_memory_space_constraint(v, pltpu.HBM) for v in (pattern, ymatrix, zmatrix)),
     )
     r1, l1 = send(r1, right), send(l1, left)
     zz = send(zz, ends)
@@ -327,11 +356,10 @@
         relay_kernel,
         (packed(R3), packed(L3)),
         [VMEM] * 2,
-        [SMEM, VMEM, ANY, VMEM, VMEM],
+        [VMEM, ANY, VMEM, VMEM],
         [],
         0,
-        (edge, zz, td, r3, l3),
-        input_output_aliases={3: 0, 4: 1},
+        (zz, td, r3, l3),
     )
     r3, l3 = send(r3, right_y), send(l3, left_y)
     square, total = jax.ShapeDtypeStruct((S, S), BF), jax.ShapeDtypeStruct((S, S), F32)
@@ -343,29 +371,48 @@
         [VMEM] * 7,
         [SMEM] + [VMEM] * 4,
         [one, full],
-        10 * S**3,
+        OWN_COST * S**3,
         (pattern, yw, zw, td, r2),
     )
-    tu, yu, yl = call(
+    lower, upper = (jax.ShapeDtypeStruct((len(v), B, B), BF) for v in (LOWER, UPPER))
+    tu, yl, yu = call(
         late_kernel,
-        (square, total, total),
+        (square, lower, upper),
         [VMEM] * 3,
         [SMEM] + [VMEM] * 6,
         [one, full],
-        50 * S**3,
+        LATE_COST * S**3,
         (pattern, yw, zw, zy, yl, e, l2),
-        input_output_aliases={4: 2},
+    )
+    zu, zd, yd = call(
+        right_kernel,
+        (upper, total, total),
+        [VMEM] * 3,
+        [SMEM] + [VMEM] * 8,
+        [one, one, one, one, full],
+        RIGHT_COST * S**3,
+        (pattern, yw, tu, zd, zu, yd, l1, l2, l3),
+        input_output_aliases={3: 1, 5: 2},
     )
     whole = jax.ShapeDtypeStruct(ymatrix.shape, BF)
-    block_rows = pltpu.VMEM(ymatrix.shape, BF)
     return call(
         last_kernel,
         (whole, whole),
         [ANY] * 2,
-        [SMEM] + [VMEM] * 15,
-        [one, one, half, half, one, one, full, block_rows, block_rows, pltpu.SemaphoreType.DMA((8,))],
+        [SMEM] + [VMEM] * 11,
+        [
+            one,
+            one,
+            one,
+            one,
+            full,
+            pltpu.VMEM((16, B, B), BF),
+            pltpu.VMEM((16, B, B), BF),
+            pltpu.VMEM((10, B, B), BF),
+            pltpu.SemaphoreType.DMA((22,)),
+        ],
         10 * S**3,
-        (pattern, yw, tl, tu, zl, zd, zu, yl, yd, yu, r1, l1, r2, l2, r3, l3),
+        (pattern, yw, tl, zl, zd, zu, yl, yd, yu, r1, r2, r3),
     )
 
 

time: 86 us -> 83.1 us (0.966)
  local copies, waits for them, and re-layouts: 3.14 us -> 0.01 us
  waiting for transfers between devices: 35.2 us -> 34.3 us
  Pallas kernels: 12.1 us -> 13 us
    unnamed x8 -> x2, local copies, waits for them, and re-layouts: 3.14 us -> 0.01 us
    ppermute x8, waiting for transfers between devices: 35.2 us -> 34.3 us  [send(): return lax.ppermute(x, AXES, pairs)]
    pallas_call x6 -> x7, Pallas kernels: 12.1 us -> 13 us  [call(): pl.pallas_call(kernel, out_shape=outs, in_specs=ins, out_specs=tuple(out_...]
  transfers between devices with their start and end apart: 8 -> 8, of which waited for: 6 -> 5; matrix products, arithmetic and copies ran while one was open for 0% -> 0% of each run, Pallas kernels for 7% -> 9%
where the time goes in v4:
time: 83.1 us; the launch traced here: 81.8 us
  waiting for transfers between devices  34.3 us (41%)
  starting transfers between devices  33.8 us (41%)
  Pallas kernels  13 us (16%)
    ppermute x8, waiting for transfers between devices, send(): return lax.ppermute(x, AXES, pairs)  34.3 us
    ppermute x8, starting transfers between devices, send(): return lax.ppermute(x, AXES, pairs)  33.8 us
    pallas_call x7, Pallas kernels, call(): pl.pallas_call(kernel, out_shape=outs, in_specs=ins, out_specs=tuple(out_...  13 us
  transfers between devices with their start and end apart: 8, of which 5 were waited for; matrix products, arithmetic and copies ran while one was open for 0% of the time, Pallas kernels for 9%

profile of v4, /device:TPU:6, one launch (start us, length us, event | category | flops | bytes accessed | tf_op | source)
XLA Modules:
  0.0 81.8 jit_solution(14905913873297988268)
XLA Ops:
  0.6 0.0 copy-start
  0.6 2.1 %shard_map.50 = (bf16[784,128]{1,0:T(8,128)(2,1)S(1)}, bf16[1296,128]{1,0:T(8,128)(2,1)S(1)}, bf16[2304,128]{1,0:T(8,128)(2,1)S(1)}, bf16[2560,128]{1,0:T(8,128)...) custom-call(s32[4,8]{1,0:T(4,128)} %pattern.9, ...), custom_call_target="tpu_custom_call" | custom-call | bytes 8167552 | tf_op jit(solution)/shard_map/pallas_call | solution.py:299
  2.8 13.6 %collective-permute-start.1 = (bf16[1296,128]{1,0:T(8,128)(2,1)S(1)}, bf16[1296,128]{1,0:T(8,128)(2,1)S(1)}, u32[]{:S(2)}, u32[]{:S(2)}) collective-permute-start(bf16[1296,128]{1,0:T(8,128)(2,1)S(1)} %get-tuple-element.31), channel_id=1, source_target_pairs={{1,0},{2,1},{3,2},{4,3},{5,4},{6,5},{7,6},{8,7},{9,8},{10,9},{11,1... | collective-permute-start | bytes 995336 | tf_op jit(solution)/shard_map/ppermute | solution.py:325
  16.4 1.9 %collective-permute-start = (bf16[784,128]{1,0:T(8,128)(2,1)S(1)}, bf16[784,128]{1,0:T(8,128)(2,1)S(1)}, u32[]{:S(2)}, u32[]{:S(2)}) collective-permute-start(bf16[784,128]{1,0:T(8,128)(2,1)S(1)} %get-tuple-element.30), channel_id=1, source_target_pairs={{0,1},{1,2},{2,3},{3,4},{4,5},{5,6},{6,7},{7,8},{8,9},{9,10},{10,1... | collective-permute-start | bytes 602120 | tf_op jit(solution)/shard_map/ppermute | solution.py:325
  18.3 2.2 %collective-permute-start.5 = (bf16[2560,128]{1,0:T(8,128)(2,1)S(1)}, bf16[2560,128]{1,0:T(8,128)(2,1)S(1)}, u32[]{:S(2)}, u32[]{:S(2)}) collective-permute-start(bf16[2560,128]{1,0:T(8,128)(2,1)S(1)} %get-tuple-element.44), channel_id=1, source_target_pairs={{7,15},{15,23},{23,31},{31,39},{39,47},{47,55},{55,63},{63,71},{71... | collective-permute-start | bytes 1966088 | tf_op jit(solution)/shard_map/ppermute | solution.py:325
  20.5 1.9 %collective-permute-start.2 = (bf16[2304,128]{1,0:T(8,128)(2,1)S(1)}, bf16[2304,128]{1,0:T(8,128)(2,1)S(1)}, u32[]{:S(2)}, u32[]{:S(2)}) collective-permute-start(bf16[2304,128]{1,0:T(8,128)(2,1)S(1)} %get-tuple-element.33), channel_id=1, source_target_pairs={{0,1},{1,2},{2,3},{3,4},{4,5},{5,6},{6,7},{7,8},{8,9},{9,10},{10,1... | collective-permute-start | bytes 1769480 | tf_op jit(solution)/shard_map/ppermute | solution.py:325
  22.4 13.3 %collective-permute-done.r1 = bf16[784,128]{1,0:T(8,128)(2,1)S(1)} collective-permute-done((bf16[784,128]{1,0:T(8,128)(2,1)S(1)}, bf16[784,128]{1,0:T(8,128)(2,1)S(1)}, u32[]{:S(2)}, u32[]{:S(2)}) %collective-permute-start) | collective-permute-done | bytes 200736 | tf_op jit(solution)/shard_map/ppermute | solution.py:325
  35.7 0.0 collective-permute-done.1.l1
  35.7 0.0 copy-done
  35.7 1.9 %shard_map.51 = (bf16[512,512]{1,0:T(8,128)(2,1)S(1)}, bf16[1280,128]{1,0:T(8,128)(2,1)S(1)}, bf16[2688,128]{1,0:T(8,128)(2,1)S(1)}) custom-call(s32[4,8]{1,0:T(4,128)S(1)} %copy-done, bf16[512,1536]{1,0:T(8,128)(2,1)S(1)} %get-tuple-element.28.yw, bf16[512,1536]{1,0:T(8,128)(2,1)S(1)} %get-tuple-element.29.zw, ...), custom_call_target="tpu_custom_call" | custom-call | flops 805306368 | bytes 5218432 | tf_op jit(solution)/shard_map/pallas_call | solution.py:299
  37.6 2.9 %collective-permute-start.4 = (bf16[2688,128]{1,0:T(8,128)(2,1)S(1)}, bf16[2688,128]{1,0:T(8,128)(2,1)S(1)}, u32[]{:S(2)}, u32[]{:S(2)}) collective-permute-start(bf16[2688,128]{1,0:T(8,128)(2,1)S(1)} %get-tuple-element.39), channel_id=1, source_target_pairs={{1,0},{2,1},{3,2},{4,3},{5,4},{6,5},{7,6},{8,7},{9,8},{10,9},{11,1... | collective-permute-start | bytes 2064392 | tf_op jit(solution)/shard_map/ppermute | solution.py:325
  40.5 2.9 %collective-permute-start.3 = (bf16[1280,128]{1,0:T(8,128)(2,1)S(1)}, bf16[1280,128]{1,0:T(8,128)(2,1)S(1)}, u32[]{:S(2)}, u32[]{:S(2)}) collective-permute-start(bf16[1280,128]{1,0:T(8,128)(2,1)S(1)} %get-tuple-element.38), channel_id=1, source_target_pairs={{0,1},{1,2},{2,3},{3,4},{4,5},{5,6},{6,7},{7,8},{8,9},{9,10},{10,1... | collective-permute-start | bytes 983048 | tf_op jit(solution)/shard_map/ppermute | solution.py:325
  43.5 8.9 %collective-permute-done.5.zz = bf16[2560,128]{1,0:T(8,128)(2,1)S(1)} collective-permute-done((bf16[2560,128]{1,0:T(8,128)(2,1)S(1)}, bf16[2560,128]{1,0:T(8,128)(2,1)S(1)}, u32[]{:S(2)}, u32[]{:S(2)}) %collective-permute-start.5) | collective-permute-done | bytes 655392 | tf_op jit(solution)/shard_map/ppermute | solution.py:325
  52.4 0.1 shard_map.54
  52.4 1.9 %collective-permute-start.7 = (bf16[2560,128]{1,0:T(8,128)(2,1)S(1)}, bf16[2560,128]{1,0:T(8,128)(2,1)S(1)}, u32[]{:S(2)}, u32[]{:S(2)}) collective-permute-start(bf16[2560,128]{1,0:T(8,128)(2,1)S(1)} %get-tuple-element.53), channel_id=1, source_target_pairs={{0,1},{1,2},{2,3},{3,4},{4,5},{5,6},{6,7},{7,0},{8,9},{9,10},{10,1... | collective-permute-start | bytes 1966088 | tf_op jit(solution)/shard_map/ppermute | solution.py:325
  54.4 6.5 %collective-permute-start.6 = (bf16[1920,128]{1,0:T(8,128)(2,1)S(1)}, bf16[1920,128]{1,0:T(8,128)(2,1)S(1)}, u32[]{:S(2)}, u32[]{:S(2)}) collective-permute-start(bf16[1920,128]{1,0:T(8,128)(2,1)S(1)} %get-tuple-element.47), channel_id=1, source_target_pairs={{1,0},{2,1},{3,2},{4,3},{5,4},{6,5},{7,6},{0,7},{9,8},{10,9},{11,1... | collective-permute-start | bytes 1474568 | tf_op jit(solution)/shard_map/ppermute | solution.py:325
  60.8 0.5 collective-permute-done.2.r2
  61.3 2.3 %shard_map.52 = (bf16[512,512]{1,0:T(8,128)(2,1)S(1)}, f32[512,512]{1,0:T(8,128)S(1)}, f32[512,512]{1,0:T(8,128)S(1)}, f32[512,512]{1,0:T(8,128)S(1)}, f32[512,5...) custom-call(s32[4,8]{1,0:T(4,128)S(1)} %copy-done, bf16[512,1536]{1,0:T(8,128)(2,1)S(1)} %get-tuple-element.28.yw, ...), custom_call_target="tpu_custom_call" | custom-call | flops 1342177280 | bytes 11075712 | tf_op jit(solution)/shard_map/pallas_call | solution.py:299
  63.7 10.6 %collective-permute-done.3.e = bf16[1280,128]{1,0:T(8,128)(2,1)S(1)} collective-permute-done((bf16[1280,128]{1,0:T(8,128)(2,1)S(1)}, bf16[1280,128]{1,0:T(8,128)(2,1)S(1)}, u32[]{:S(2)}, u32[]{:S(2)}) %collective-permute-start.3) | collective-permute-done | bytes 327712 | tf_op jit(solution)/shard_map/ppermute | solution.py:325
  74.3 0.0 collective-permute-done.4.l2
  74.3 1.3 %shard_map.53 = (bf16[512,512]{1,0:T(8,128)(2,1)S(1)}, bf16[10,128,128]{2,1,0:T(8,128)(2,1)S(1)}, bf16[6,128,128]{2,1,0:T(8,128)(2,1)S(1)}) custom-call(s32[4,8]{1,0:T(4,128)S(1)} %copy-done, bf16[512,1536]{1,0:T(8,128)(2,1)S(1)} %get-tuple-element.28.yw, bf16[512,1536]{1,0:T(8,128)(2,1)S(1)} %get-tuple-element.29.zw, f32[512,512]{1,0:T(8,128)S(1)} %get-tuple-element.36.zy, ...), custom_call_target="tpu_custom_call" | custom-call | flops 4697620480 | bytes 7307392 | tf_op jit(solution)/shard_map/pallas_call | solution.py:299
  75.6 0.0 collective-permute-done.6.l3
  75.6 1.9 %shard_map.55 = (bf16[6,128,128]{2,1,0:T(8,128)(2,1)S(1)}, f32[512,512]{1,0:T(8,128)S(1)}, f32[512,512]{1,0:T(8,128)S(1)}) custom-call(s32[4,8]{1,0:T(4,128)S(1)} %copy-done, bf16[512,1536]{1,0:T(8,128)(2,1)S(1)} %get-tuple-element.28.yw, bf16[512,512]{1,0:T(8,128)(2,1)S(1)} %get-tuple-element.40.tu, ...), custom_call_target="tpu_custom_call", output_to_operand_aliasing={{1}: (3, {}), {2}: (5, {})} | custom-call | flops 671088640 | bytes 9048192 | tf_op jit(solution)/shard_map/pallas_call | solution.py:299
  77.5 1.0 %collective-permute-done.7.r3 = bf16[2560,128]{1,0:T(8,128)(2,1)S(1)} collective-permute-done((bf16[2560,128]{1,0:T(8,128)(2,1)S(1)}, bf16[2560,128]{1,0:T(8,128)(2,1)S(1)}, u32[]{:S(2)}, u32[]{:S(2)}) %collective-permute-start.7) | collective-permute-done | bytes 655392 | tf_op jit(solution)/shard_map/ppermute | solution.py:325
  78.5 3.3 %shard_map.56 = (bf16[4,8,128,128]{3,2,1,0:T(8,128)(2,1)}, bf16[4,8,128,128]{3,2,1,0:T(8,128)(2,1)}) custom-call(s32[4,8]{1,0:T(4,128)S(1)} %copy-done, bf16[512,1536]{1,0:T(8,128)(2,1)S(1)} %get-tuple-element.28.yw, bf16[512,512]{1,0:T(8,128)(2,1)S(1)} %get-tuple-element.34.tl, f32[512,512]{1,0:T(8,128)S(1)} %get-tuple-element.35.zl, ...), custom_call_target="tpu_custom_call" | custom-call | flops 1342177280 | bytes 9506944 | tf_op jit(solution)/shard_map/pallas_call | solution.py:299
Async XLA Ops:
  0.6 35.1 %copy-start = (s32[4,8]{1,0:T(4,128)S(1)}, s32[4,8]{1,0:T(4,128)}, u32[]{:S(2)}) copy-start(s32[4,8]{1,0:T(4,128)} %pattern.9) | copy-start | bytes 388
  2.8 32.9 %collective-permute-start.1 = (bf16[1296,128]{1,0:T(8,128)(2,1)S(1)}, bf16[1296,128]{1,0:T(8,128)(2,1)S(1)}, u32[]{:S(2)}, u32[]{:S(2)}) collective-permute-start(bf16[1296,128]{1,0:T(8,128)(2,1)S(1)} %get-tuple-element.31), channel_id=1, source_target_pairs={{1,0},{2,1},{3,2},{4,3},{5,4},{6,5},{7,6},{8,7},{9,8},{10,9},{11,1... | collective-permute-start | bytes 995336 | tf_op jit(solution)/shard_map/ppermute | solution.py:325
  16.4 19.3 %collective-permute-start = (bf16[784,128]{1,0:T(8,128)(2,1)S(1)}, bf16[784,128]{1,0:T(8,128)(2,1)S(1)}, u32[]{:S(2)}, u32[]{:S(2)}) collective-permute-start(bf16[784,128]{1,0:T(8,128)(2,1)S(1)} %get-tuple-element.30), channel_id=1, source_target_pairs={{0,1},{1,2},{2,3},{3,4},{4,5},{5,6},{6,7},{7,8},{8,9},{9,10},{10,1... | collective-permute-start | bytes 602120 | tf_op jit(solution)/shard_map/ppermute | solution.py:325
  18.3 34.1 %collective-permute-start.5 = (bf16[2560,128]{1,0:T(8,128)(2,1)S(1)}, bf16[2560,128]{1,0:T(8,128)(2,1)S(1)}, u32[]{:S(2)}, u32[]{:S(2)}) collective-permute-start(bf16[2560,128]{1,0:T(8,128)(2,1)S(1)} %get-tuple-element.44), channel_id=1, source_target_pairs={{7,15},{15,23},{23,31},{31,39},{39,47},{47,55},{55,63},{63,71},{71... | collective-permute-start | bytes 1966088 | tf_op jit(solution)/shard_map/ppermute | solution.py:325
  20.5 40.9 %collective-permute-start.2 = (bf16[2304,128]{1,0:T(8,128)(2,1)S(1)}, bf16[2304,128]{1,0:T(8,128)(2,1)S(1)}, u32[]{:S(2)}, u32[]{:S(2)}) collective-permute-start(bf16[2304,128]{1,0:T(8,128)(2,1)S(1)} %get-tuple-element.33), channel_id=1, source_target_pairs={{0,1},{1,2},{2,3},{3,4},{4,5},{5,6},{6,7},{7,8},{8,9},{9,10},{10,1... | collective-permute-start | bytes 1769480 | tf_op jit(solution)/shard_map/ppermute | solution.py:325
  37.6 36.7 %collective-permute-start.4 = (bf16[2688,128]{1,0:T(8,128)(2,1)S(1)}, bf16[2688,128]{1,0:T(8,128)(2,1)S(1)}, u32[]{:S(2)}, u32[]{:S(2)}) collective-permute-start(bf16[2688,128]{1,0:T(8,128)(2,1)S(1)} %get-tuple-element.39), channel_id=1, source_target_pairs={{1,0},{2,1},{3,2},{4,3},{5,4},{6,5},{7,6},{8,7},{9,8},{10,9},{11,1... | collective-permute-start | bytes 2064392 | tf_op jit(solution)/shard_map/ppermute | solution.py:325
  40.5 33.7 %collective-permute-start.3 = (bf16[1280,128]{1,0:T(8,128)(2,1)S(1)}, bf16[1280,128]{1,0:T(8,128)(2,1)S(1)}, u32[]{:S(2)}, u32[]{:S(2)}) collective-permute-start(bf16[1280,128]{1,0:T(8,128)(2,1)S(1)} %get-tuple-element.38), channel_id=1, source_target_pairs={{0,1},{1,2},{2,3},{3,4},{4,5},{5,6},{6,7},{7,8},{8,9},{9,10},{10,1... | collective-permute-start | bytes 983048 | tf_op jit(solution)/shard_map/ppermute | solution.py:325
  52.4 26.1 %collective-permute-start.7 = (bf16[2560,128]{1,0:T(8,128)(2,1)S(1)}, bf16[2560,128]{1,0:T(8,128)(2,1)S(1)}, u32[]{:S(2)}, u32[]{:S(2)}) collective-permute-start(bf16[2560,128]{1,0:T(8,128)(2,1)S(1)} %get-tuple-element.53), channel_id=1, source_target_pairs={{0,1},{1,2},{2,3},{3,4},{4,5},{5,6},{6,7},{7,0},{8,9},{9,10},{10,1... | collective-permute-start | bytes 1966088 | tf_op jit(solution)/shard_map/ppermute | solution.py:325
  54.4 21.2 %collective-permute-start.6 = (bf16[1920,128]{1,0:T(8,128)(2,1)S(1)}, bf16[1920,128]{1,0:T(8,128)(2,1)S(1)}, u32[]{:S(2)}, u32[]{:S(2)}) collective-permute-start(bf16[1920,128]{1,0:T(8,128)(2,1)S(1)} %get-tuple-element.47), channel_id=1, source_target_pairs={{1,0},{2,1},{3,2},{4,3},{5,4},{6,5},{7,6},{0,7},{9,8},{10,9},{11,1... | collective-permute-start | bytes 1474568 | tf_op jit(solution)/shard_map/ppermute | solution.py:325

commit v5 on v4

--- a/solution.py
+++ b/solution.py
@@ -27,7 +27,7 @@
 L_TOP = [p for p in LOWER if p[0] < 3]
 R_REST = of("yD", FULL) + of("zU", UPPER) + of("zD", FULL)
 L_REST = of("yD", [(r, c) for r in range(3) for c in range(3)]) + of("zL", L_TOP) + of("zD", FULL[:12])
-R2, R3 = R_REST[:18], R_REST[18:]
+R2, R3 = R_REST[:19], R_REST[19:]
 L2, L3 = of("sum", UPPER) + L_REST[:15], L_REST[15:]
 COLUMN = {"L": 0, "D": S, "U": 2 * S}
 QUADS = {
@@ -90,8 +90,24 @@
     return block if flag is True else jnp.where(flag, block, jnp.zeros_like(block))
 
 
-def pack_kernel(pattern_in, y, z, r1, l1, r2, r3, l3, zz, yw, zw, yin, zin, pattern, sems):
-    place = lax.rem(lax.axis_index("col"), RING)
+def widen(pattern, wide, source, ready):
+    for r in range(4):
+        for c in range(12):
+            if not r <= c < r + 8:
+                wide[rows(r), rows(c)] = jnp.zeros((B, B), BF)
+        ready(r)
+        for d in range(8):
+            k = True if d == 4 else pattern[r, d] == 1
+            wide[rows(r), rows(r + d)] = masked(k, source[r, d])
+
+
+def fill(message, ref, yw, zw):
+    for i, (name, r, c) in enumerate(message):
+        wide = yw if name[0] == "y" else zw
+        ref[rows(i), :] = wide[rows(r), pl.ds(COLUMN[name[1]] + c * B, B)]
+
+
+def first_kernel(pattern_in, y, z, r1, l1, yw, zin, yin, pattern, sems):
     copies = [pltpu.make_async_copy(pattern_in, pattern, sems.at[8])]
     for i, (source, target) in enumerate(((y, yin), (z, zin))):
         for r in range(4):
@@ -99,39 +115,32 @@
     for copy in copies:
         copy.start()
     copies[0].wait()
-    for i, (wide, source) in enumerate(((yw, yin), (zw, zin))):
-        for r in range(4):
-            for c in range(12):
-                if not r <= c < r + 8:
-                    wide[rows(r), rows(c)] = jnp.zeros((B, B), BF)
-            copies[1 + i * 4 + r].wait()
-            for d in range(8):
-                k = True if d == 4 else pattern[r, d] == 1
-                wide[rows(r), rows(r + d)] = masked(k, source[r, d])
-
-    def fill(message, ref):
-        for i, (name, r, c) in enumerate(message):
-            wide = yw if name[0] == "y" else zw
-            ref[rows(i), :] = wide[rows(r), pl.ds(COLUMN[name[1]] + c * B, B)]
-
-    for message, ref in ((R1, r1), (L1, l1), (R2, r2), (R3, r3), (L3, l3)):
-        fill(message, ref)
-
-    @pl.when(place == 0)
-    def _():
-        fill(L3, zz)
-
-    @pl.when(place == RING - 1)
-    def _():
-        fill(R3, zz)
-
+    widen(pattern, yw, yin, lambda r: copies[1 + r].wait())
     line = lax.broadcasted_iota(jnp.int32, (16, B), 0)
     for message, ref in ((R1, r1), (L1, l1)):
+        fill(message, ref, yw, None)
         tile = jnp.zeros((16, B), F32)
         for i, (name, r, c) in enumerate(message):
             k = keep(pattern, name[1], r, c)
             tile = jnp.where(line == i, 1.0 if k is True else jnp.where(k, 1.0, 0.0), tile)
         ref[pl.ds(len(message) * B, 16), :] = tile.astype(BF)
+    for copy in copies[5:]:
+        copy.wait()
+
+
+def second_kernel(pattern, yw, zin, r2, r3, l3, zz, zw):
+    place = lax.rem(lax.axis_index("col"), RING)
+    widen(pattern, zw, zin, lambda r: None)
+    for message, ref in ((R2, r2), (R3, r3), (L3, l3)):
+        fill(message, ref, yw, zw)
+
+    @pl.when(place == 0)
+    def _():
+        fill(L3, zz, yw, zw)
+
+    @pl.when(place == RING - 1)
+    def _():
+        fill(R3, zz, yw, zw)
 
 
 def middle_kernel(pattern, yw, zw, r1, l1, td, e, l, yu, yl, acc):
@@ -206,7 +215,7 @@
         block = total[rows(r), rows(c)]
         if extra is not None:
             block = block + extra[rows(i), :].astype(F32)
-        out[i] = masked(keep(pattern, part, r, c), block).astype(BF)
+        out[i] = masked(keep(pattern, part, r, c), block.astype(BF))
 
 
 def late_kernel(pattern, yw, zw, zy, yl, e, l2, tu, yl_out, yu_out, yc, acc):
@@ -325,19 +334,28 @@
         return lax.ppermute(x, AXES, pairs)
 
     wide = jax.ShapeDtypeStruct((S, 3 * S), BF)
-    r1, l1, r2, r3, l3, zz, yw, zw = call(
-        pack_kernel,
-        (packed(R1, True), packed(L1, True)) + tuple(packed(m) for m in (R2, R3, L3, max(R3, L3, key=len))) + (wide, wide),
-        [VMEM] * 8,
+    band = jax.ShapeDtypeStruct(ymatrix.shape, BF)
+    r1, l1, yw, zin = call(
+        first_kernel,
+        (packed(R1, True), packed(L1, True), wide, band),
+        [VMEM] * 4,
         [HBM] * 3,
         [
-            pltpu.VMEM(ymatrix.shape, BF),
             pltpu.VMEM(ymatrix.shape, BF),
             pltpu.SMEM(pattern.shape, jnp.int32),
             pltpu.SemaphoreType.DMA((9,)),
         ],
         0,
         tuple(pltpu.with_memory_space_constraint(v, pltpu.HBM) for v in (pattern, ymatrix, zmatrix)),
+    )
+    r2, r3, l3, zz, zw = call(
+        second_kernel,
+        tuple(packed(m) for m in (R2, R3, L3, max(R3, L3, key=len))) + (wide,),
+        [VMEM] * 5,
+        [SMEM, VMEM, VMEM],
+        [],
+        0,
+        (pattern, yw, zin),
     )
     r1, l1 = send(r1, right), send(l1, left)
     zz = send(zz, ends)

time: 83.1 us -> 83 us (level)
  waiting for transfers between devices: 34.3 us -> 33.4 us
    ppermute x8, waiting for transfers between devices: 34.3 us -> 33.4 us  [send(): return lax.ppermute(x, AXES, pairs)]
    pallas_call x7 -> x8, Pallas kernels: 13 us -> 13.7 us  [call(): pl.pallas_call(kernel, out_shape=outs, in_specs=ins, out_specs=tuple(out_...]
  transfers between devices with their start and end apart: 8 -> 8, of which waited for: 5 -> 4; matrix products, arithmetic and copies ran while one was open for 0% -> 0% of each run, Pallas kernels for 9% -> 11%
where the time goes in v5:
time: 83 us; the launch traced here: 81.6 us
  starting transfers between devices  33.8 us (41%)
  waiting for transfers between devices  33.4 us (40%)
  Pallas kernels  13.7 us (17%)
    ppermute x8, starting transfers between devices, send(): return lax.ppermute(x, AXES, pairs)  33.8 us
    ppermute x8, waiting for transfers between devices, send(): return lax.ppermute(x, AXES, pairs)  33.4 us
    pallas_call x8, Pallas kernels, call(): pl.pallas_call(kernel, out_shape=outs, in_specs=ins, out_specs=tuple(out_...  13.7 us
  transfers between devices with their start and end apart: 8, of which 4 were waited for; matrix products, arithmetic and copies ran while one was open for 0% of the time, Pallas kernels for 11%

profile of v5, /device:TPU:6, one launch (start us, length us, event | category | flops | bytes accessed | tf_op | source)
XLA Modules:
  0.0 81.6 jit_solution(17516682662681360411)
XLA Ops:
  0.6 0.0 copy-start
  0.6 1.6 %shard_map.50 = (bf16[784,128]{1,0:T(8,128)(2,1)S(1)}, bf16[1296,128]{1,0:T(8,128)(2,1)S(1)}, bf16[512,1536]{1,0:T(8,128)(2,1)S(1)}, bf16[4,8,128,128]{3,2,1,0:T(8,128)(2,1)S(1)}) custom-call(s32[4,8]{1,0:T(4,128)} %pattern.11, bf16[4,8,128,128]{3,2,1,0:T(8,128)(2,1)} %y.1, bf16[4,8,128,128]{3,2,1,0:T(8,128)(2,1)} %z.1), custom_call_target="tpu_custom_call" | custom-call | bytes 5251200 | tf_op jit(solution)/shard_map/pallas_call | solution.py:308
  2.2 13.5 %collective-permute-start.1 = (bf16[1296,128]{1,0:T(8,128)(2,1)S(1)}, bf16[1296,128]{1,0:T(8,128)(2,1)S(1)}, u32[]{:S(2)}, u32[]{:S(2)}) collective-permute-start(bf16[1296,128]{1,0:T(8,128)(2,1)S(1)} %get-tuple-element.33), channel_id=1, source_target_pairs={{1,0},{2,1},{3,2},{4,3},{5,4},{6,5},{7,6},{8,7},{9,8},{10,9},{11,1... | collective-permute-start | bytes 995336 | tf_op jit(solution)/shard_map/ppermute | solution.py:334
  15.8 1.9 %collective-permute-start = (bf16[784,128]{1,0:T(8,128)(2,1)S(1)}, bf16[784,128]{1,0:T(8,128)(2,1)S(1)}, u32[]{:S(2)}, u32[]{:S(2)}) collective-permute-start(bf16[784,128]{1,0:T(8,128)(2,1)S(1)} %get-tuple-element.32), channel_id=1, source_target_pairs={{0,1},{1,2},{2,3},{3,4},{4,5},{5,6},{6,7},{7,8},{8,9},{9,10},{10,1... | collective-permute-start | bytes 602120 | tf_op jit(solution)/shard_map/ppermute | solution.py:334
  17.7 0.0 copy-done
  17.7 1.2 %shard_map.51 = (bf16[2432,128]{1,0:T(8,128)(2,1)S(1)}, bf16[2432,128]{1,0:T(8,128)(2,1)S(1)}, bf16[1920,128]{1,0:T(8,128)(2,1)S(1)}, bf16[2432,128]{1,0:T(8,128)(2,1)S(1)}, bf16[512,1536]{1,0:T(8,128)(2,1)S(1)}) custom-call(s32[4,8]{1,0:T(4,128)S(1)} %copy-done, bf16[512,1536]{1,0:T(8,128)(2,1)S(1)} %get-tuple-element.29.yw, ...), custom_call_target="tpu_custom_call" | custom-call | bytes 6553728 | tf_op jit(solution)/shard_map/pallas_call | solution.py:308
  19.0 1.9 %collective-permute-start.2 = (bf16[2432,128]{1,0:T(8,128)(2,1)S(1)}, bf16[2432,128]{1,0:T(8,128)(2,1)S(1)}, u32[]{:S(2)}, u32[]{:S(2)}) collective-permute-start(bf16[2432,128]{1,0:T(8,128)(2,1)S(1)} %get-tuple-element.35), channel_id=1, source_target_pairs={{0,1},{1,2},{2,3},{3,4},{4,5},{5,6},{6,7},{7,8},{8,9},{9,10},{10,1... | collective-permute-start | bytes 1867784 | tf_op jit(solution)/shard_map/ppermute | solution.py:334
  20.9 2.2 %collective-permute-start.5 = (bf16[2432,128]{1,0:T(8,128)(2,1)S(1)}, bf16[2432,128]{1,0:T(8,128)(2,1)S(1)}, u32[]{:S(2)}, u32[]{:S(2)}) collective-permute-start(bf16[2432,128]{1,0:T(8,128)(2,1)S(1)} %get-tuple-element.46), channel_id=1, source_target_pairs={{7,15},{15,23},{23,31},{31,39},{39,47},{47,55},{55,63},{63,71},{71... | collective-permute-start | bytes 1867784 | tf_op jit(solution)/shard_map/ppermute | solution.py:334
  23.1 12.0 %collective-permute-done.r1 = bf16[784,128]{1,0:T(8,128)(2,1)S(1)} collective-permute-done((bf16[784,128]{1,0:T(8,128)(2,1)S(1)}, bf16[784,128]{1,0:T(8,128)(2,1)S(1)}, u32[]{:S(2)}, u32[]{:S(2)}) %collective-permute-start) | collective-permute-done | bytes 200736 | tf_op jit(solution)/shard_map/ppermute | solution.py:334
  35.1 0.0 collective-permute-done.1.l1
  35.1 1.9 %shard_map.52 = (bf16[512,512]{1,0:T(8,128)(2,1)S(1)}, bf16[1280,128]{1,0:T(8,128)(2,1)S(1)}, bf16[2688,128]{1,0:T(8,128)(2,1)S(1)}) custom-call(s32[4,8]{1,0:T(4,128)S(1)} %copy-done, bf16[512,1536]{1,0:T(8,128)(2,1)S(1)} %get-tuple-element.29.yw, bf16[512,1536]{1,0:T(8,128)(2,1)S(1)} %get-tuple-element.31.zw, ...), custom_call_target="tpu_custom_call" | custom-call | flops 805306368 | bytes 5218432 | tf_op jit(solution)/shard_map/pallas_call | solution.py:308
  37.0 2.9 %collective-permute-start.4 = (bf16[2688,128]{1,0:T(8,128)(2,1)S(1)}, bf16[2688,128]{1,0:T(8,128)(2,1)S(1)}, u32[]{:S(2)}, u32[]{:S(2)}) collective-permute-start(bf16[2688,128]{1,0:T(8,128)(2,1)S(1)} %get-tuple-element.41), channel_id=1, source_target_pairs={{1,0},{2,1},{3,2},{4,3},{5,4},{6,5},{7,6},{8,7},{9,8},{10,9},{11,1... | collective-permute-start | bytes 2064392 | tf_op jit(solution)/shard_map/ppermute | solution.py:334
  40.0 2.9 %collective-permute-start.3 = (bf16[1280,128]{1,0:T(8,128)(2,1)S(1)}, bf16[1280,128]{1,0:T(8,128)(2,1)S(1)}, u32[]{:S(2)}, u32[]{:S(2)}) collective-permute-start(bf16[1280,128]{1,0:T(8,128)(2,1)S(1)} %get-tuple-element.40), channel_id=1, source_target_pairs={{0,1},{1,2},{2,3},{3,4},{4,5},{5,6},{6,7},{7,8},{8,9},{9,10},{10,1... | collective-permute-start | bytes 983048 | tf_op jit(solution)/shard_map/ppermute | solution.py:334
  42.9 10.7 %collective-permute-done.5.zz = bf16[2432,128]{1,0:T(8,128)(2,1)S(1)} collective-permute-done((bf16[2432,128]{1,0:T(8,128)(2,1)S(1)}, bf16[2432,128]{1,0:T(8,128)(2,1)S(1)}, u32[]{:S(2)}, u32[]{:S(2)}) %collective-permute-start.5) | collective-permute-done | bytes 622624 | tf_op jit(solution)/shard_map/ppermute | solution.py:334
  53.6 0.1 shard_map.55
  53.6 6.5 %collective-permute-start.6 = (bf16[1920,128]{1,0:T(8,128)(2,1)S(1)}, bf16[1920,128]{1,0:T(8,128)(2,1)S(1)}, u32[]{:S(2)}, u32[]{:S(2)}) collective-permute-start(bf16[1920,128]{1,0:T(8,128)(2,1)S(1)} %get-tuple-element.49), channel_id=1, source_target_pairs={{1,0},{2,1},{3,2},{4,3},{5,4},{6,5},{7,6},{0,7},{9,8},{10,9},{11,1... | collective-permute-start | bytes 1474568 | tf_op jit(solution)/shard_map/ppermute | solution.py:334
  60.1 1.9 %collective-permute-start.7 = (bf16[2432,128]{1,0:T(8,128)(2,1)S(1)}, bf16[2432,128]{1,0:T(8,128)(2,1)S(1)}, u32[]{:S(2)}, u32[]{:S(2)}) collective-permute-start(bf16[2432,128]{1,0:T(8,128)(2,1)S(1)} %get-tuple-element.55), channel_id=1, source_target_pairs={{0,1},{1,2},{2,3},{3,4},{4,5},{5,6},{6,7},{7,0},{8,9},{9,10},{10,1... | collective-permute-start | bytes 1867784 | tf_op jit(solution)/shard_map/ppermute | solution.py:334
  62.1 0.1 collective-permute-done.2.r2
  62.1 2.3 %shard_map.53 = (bf16[512,512]{1,0:T(8,128)(2,1)S(1)}, f32[512,512]{1,0:T(8,128)S(1)}, f32[512,512]{1,0:T(8,128)S(1)}, f32[512,512]{1,0:T(8,128)S(1)}, f32[512,5...) custom-call(s32[4,8]{1,0:T(4,128)S(1)} %copy-done, bf16[512,1536]{1,0:T(8,128)(2,1)S(1)} %get-tuple-element.29.yw, ...), custom_call_target="tpu_custom_call" | custom-call | flops 1342177280 | bytes 11108480 | tf_op jit(solution)/shard_map/pallas_call | solution.py:308
  64.5 10.6 %collective-permute-done.3.e = bf16[1280,128]{1,0:T(8,128)(2,1)S(1)} collective-permute-done((bf16[1280,128]{1,0:T(8,128)(2,1)S(1)}, bf16[1280,128]{1,0:T(8,128)(2,1)S(1)}, u32[]{:S(2)}, u32[]{:S(2)}) %collective-permute-start.3) | collective-permute-done | bytes 327712 | tf_op jit(solution)/shard_map/ppermute | solution.py:334
  75.1 0.0 collective-permute-done.4.l2
  75.1 1.3 %shard_map.54 = (bf16[512,512]{1,0:T(8,128)(2,1)S(1)}, bf16[10,128,128]{2,1,0:T(8,128)(2,1)S(1)}, bf16[6,128,128]{2,1,0:T(8,128)(2,1)S(1)}) custom-call(s32[4,8]{1,0:T(4,128)S(1)} %copy-done, bf16[512,1536]{1,0:T(8,128)(2,1)S(1)} %get-tuple-element.29.yw, bf16[512,1536]{1,0:T(8,128)(2,1)S(1)} %get-tuple-element.31.zw, f32[512,512]{1,0:T(8,128)S(1)} %get-tuple-element.38.zy, ...), custom_call_target="tpu_custom_call" | custom-call | flops 4697620480 | bytes 7307392 | tf_op jit(solution)/shard_map/pallas_call | solution.py:308
  76.4 0.0 collective-permute-done.6.l3
  76.4 1.9 %shard_map.56 = (bf16[6,128,128]{2,1,0:T(8,128)(2,1)S(1)}, f32[512,512]{1,0:T(8,128)S(1)}, f32[512,512]{1,0:T(8,128)S(1)}) custom-call(s32[4,8]{1,0:T(4,128)S(1)} %copy-done, bf16[512,1536]{1,0:T(8,128)(2,1)S(1)} %get-tuple-element.29.yw, bf16[512,512]{1,0:T(8,128)(2,1)S(1)} %get-tuple-element.42.tu, ...), custom_call_target="tpu_custom_call", output_to_operand_aliasing={{1}: (3, {}), {2}: (5, {})} | custom-call | flops 671088640 | bytes 9048192 | tf_op jit(solution)/shard_map/pallas_call | solution.py:308
  78.3 0.0 collective-permute-done.7.r3
  78.3 3.3 %shard_map.57 = (bf16[4,8,128,128]{3,2,1,0:T(8,128)(2,1)}, bf16[4,8,128,128]{3,2,1,0:T(8,128)(2,1)}) custom-call(s32[4,8]{1,0:T(4,128)S(1)} %copy-done, bf16[512,1536]{1,0:T(8,128)(2,1)S(1)} %get-tuple-element.29.yw, bf16[512,512]{1,0:T(8,128)(2,1)S(1)} %get-tuple-element.36.tl, f32[512,512]{1,0:T(8,128)S(1)} %get-tuple-element.37.zl, ...), custom_call_target="tpu_custom_call" | custom-call | flops 1342177280 | bytes 9506944 | tf_op jit(solution)/shard_map/pallas_call | solution.py:308
Async XLA Ops:
  0.6 17.1 %copy-start = (s32[4,8]{1,0:T(4,128)S(1)}, s32[4,8]{1,0:T(4,128)}, u32[]{:S(2)}) copy-start(s32[4,8]{1,0:T(4,128)} %pattern.11) | copy-start | bytes 388
  2.2 32.9 %collective-permute-start.1 = (bf16[1296,128]{1,0:T(8,128)(2,1)S(1)}, bf16[1296,128]{1,0:T(8,128)(2,1)S(1)}, u32[]{:S(2)}, u32[]{:S(2)}) collective-permute-start(bf16[1296,128]{1,0:T(8,128)(2,1)S(1)} %get-tuple-element.33), channel_id=1, source_target_pairs={{1,0},{2,1},{3,2},{4,3},{5,4},{6,5},{7,6},{8,7},{9,8},{10,9},{11,1... | collective-permute-start | bytes 995336 | tf_op jit(solution)/shard_map/ppermute | solution.py:334
  15.8 19.3 %collective-permute-start = (bf16[784,128]{1,0:T(8,128)(2,1)S(1)}, bf16[784,128]{1,0:T(8,128)(2,1)S(1)}, u32[]{:S(2)}, u32[]{:S(2)}) collective-permute-start(bf16[784,128]{1,0:T(8,128)(2,1)S(1)} %get-tuple-element.32), channel_id=1, source_target_pairs={{0,1},{1,2},{2,3},{3,4},{4,5},{5,6},{6,7},{7,8},{8,9},{9,10},{10,1... | collective-permute-start | bytes 602120 | tf_op jit(solution)/shard_map/ppermute | solution.py:334
  19.0 43.2 %collective-permute-start.2 = (bf16[2432,128]{1,0:T(8,128)(2,1)S(1)}, bf16[2432,128]{1,0:T(8,128)(2,1)S(1)}, u32[]{:S(2)}, u32[]{:S(2)}) collective-permute-start(bf16[2432,128]{1,0:T(8,128)(2,1)S(1)} %get-tuple-element.35), channel_id=1, source_target_pairs={{0,1},{1,2},{2,3},{3,4},{4,5},{5,6},{6,7},{7,8},{8,9},{9,10},{10,1... | collective-permute-start | bytes 1867784 | tf_op jit(solution)/shard_map/ppermute | solution.py:334
  20.9 32.7 %collective-permute-start.5 = (bf16[2432,128]{1,0:T(8,128)(2,1)S(1)}, bf16[2432,128]{1,0:T(8,128)(2,1)S(1)}, u32[]{:S(2)}, u32[]{:S(2)}) collective-permute-start(bf16[2432,128]{1,0:T(8,128)(2,1)S(1)} %get-tuple-element.46), channel_id=1, source_target_pairs={{7,15},{15,23},{23,31},{31,39},{39,47},{47,55},{55,63},{63,71},{71... | collective-permute-start | bytes 1867784 | tf_op jit(solution)/shard_map/ppermute | solution.py:334
  37.0 38.1 %collective-permute-start.4 = (bf16[2688,128]{1,0:T(8,128)(2,1)S(1)}, bf16[2688,128]{1,0:T(8,128)(2,1)S(1)}, u32[]{:S(2)}, u32[]{:S(2)}) collective-permute-start(bf16[2688,128]{1,0:T(8,128)(2,1)S(1)} %get-tuple-element.41), channel_id=1, source_target_pairs={{1,0},{2,1},{3,2},{4,3},{5,4},{6,5},{7,6},{8,7},{9,8},{10,9},{11,1... | collective-permute-start | bytes 2064392 | tf_op jit(solution)/shard_map/ppermute | solution.py:334
  40.0 35.1 %collective-permute-start.3 = (bf16[1280,128]{1,0:T(8,128)(2,1)S(1)}, bf16[1280,128]{1,0:T(8,128)(2,1)S(1)}, u32[]{:S(2)}, u32[]{:S(2)}) collective-permute-start(bf16[1280,128]{1,0:T(8,128)(2,1)S(1)} %get-tuple-element.40), channel_id=1, source_target_pairs={{0,1},{1,2},{2,3},{3,4},{4,5},{5,6},{6,7},{7,8},{8,9},{9,10},{10,1... | collective-permute-start | bytes 983048 | tf_op jit(solution)/shard_map/ppermute | solution.py:334
  53.6 22.8 %collective-permute-start.6 = (bf16[1920,128]{1,0:T(8,128)(2,1)S(1)}, bf16[1920,128]{1,0:T(8,128)(2,1)S(1)}, u32[]{:S(2)}, u32[]{:S(2)}) collective-permute-start(bf16[1920,128]{1,0:T(8,128)(2,1)S(1)} %get-tuple-element.49), channel_id=1, source_target_pairs={{1,0},{2,1},{3,2},{4,3},{5,4},{6,5},{7,6},{0,7},{9,8},{10,9},{11,1... | collective-permute-start | bytes 1474568 | tf_op jit(solution)/shard_map/ppermute | solution.py:334
  60.1 18.2 %collective-permute-start.7 = (bf16[2432,128]{1,0:T(8,128)(2,1)S(1)}, bf16[2432,128]{1,0:T(8,128)(2,1)S(1)}, u32[]{:S(2)}, u32[]{:S(2)}) collective-permute-start(bf16[2432,128]{1,0:T(8,128)(2,1)S(1)} %get-tuple-element.55), channel_id=1, source_target_pairs={{0,1},{1,2},{2,3},{3,4},{4,5},{5,6},{6,7},{7,0},{8,9},{9,10},{10,1... | collective-permute-start | bytes 1867784 | tf_op jit(solution)/shard_map/ppermute | solution.py:334
